TPU v7x, 32 devices: a whole 2x2x4 slice. The times are simulated.
32 devices in a mesh: pipe: 4 (over z), expert: 8 (over y, x, core).
Axes of the slice: x: 2, y: 2, z: 4, core: 2. Of those that a mesh axis runs over, the one named last changes fastest.
Arguments:
- tokens_up: bfloat16 [2, 256, 3584], P(None, 'expert'), may hold values from -6 to 6
- tokens_down: bfloat16 [2, 256, 3584], P(None, 'expert'), may hold values from -6 to 6
- norm_gain: float32 [4, 3584], P('pipe'), may hold values from 0.1 to 1.9
- w_gate: bfloat16 [4, 3584, 8192], P('pipe', None, 'expert'), may hold values from -0.09375 to 0.09375
- w_up: bfloat16 [4, 3584, 8192], P('pipe', None, 'expert'), may hold values from -0.09375 to 0.09375
- w_down: bfloat16 [4, 8192, 3584], P('pipe', 'expert'), may hold values from -0.1875 to 0.1875
- route_up: int32 [4, 2, 256, 2], P('pipe', None, 'expert'), may hold values from 0 to 7, all different within a row; in each aligned block of 32 rows (0 to 31, 32 to 63, ..., all dimensions but the last counted through in order) at most 16 rows name the same one
- route_down: int32 [4, 2, 256, 2], P('pipe', None, 'expert'), may hold values from 0 to 7, all different within a row; in each aligned block of 32 rows (0 to 31, 32 to 63, ..., all dimensions but the last counted through in order) at most 16 rows name the same one
- gate_up: float32 [4, 2, 256, 2], P('pipe', None, 'expert'), may hold values from 0.1 to 1
- gate_down: float32 [4, 2, 256, 2], P('pipe', None, 'expert'), may hold values from 0.1 to 1
Outputs:
- acts_up: bfloat16 [4, 2, 256, 3584], P('pipe', None, 'expert')
- acts_down: bfloat16 [4, 2, 256, 3584], P('pipe', None, 'expert')
Inputs may be any that keep to these rules, and one draw needn't show every extreme that they name: `route_up`: within the 32 rows of one device at one section and micro-batch (aligned blocks of 32 tokens), the 2 experts of a token differ, no expert is named more than 16 times, and in some block an expert is named exactly 16 times. `route_down`: within the 32 rows of one device at one section and micro-batch (aligned blocks of 32 tokens), the 2 experts of a token differ, no expert is named more than 16 times, and in some block an expert is named exactly 16 times.
All inputs are finite; a program needn't handle non-finite values.
Results may differ from a plain program's by a relative error of at most 0.0085.
Values may be sent and summed in bfloat16 or wider, within the bound.
No kernel may reach another device: no remote copies, remote signals or barrier semaphores. Data moves between devices by JAX's collectives and lax.ppermute only.
A program may use at most 128 MiB of HBM per device.

v0:
```python
import functools

import jax
import jax.numpy as jnp
from jax import lax
from jax.experimental import pallas as pl
from jax.experimental.pallas import tpu as pltpu
from jax.sharding import PartitionSpec as P

BLOCKS = 2
HIDS = 256


def spans(size, step):
    return [slice(at, at + step) for at in range(0, size, step)]


def expert_kernel(count, *refs):
    blocks, refs = refs[:count], refs[count:]
    pick_ref, put_ref, weight_ref, gain_ref, gate_hbm, up_hbm, down_hbm = refs[:7]
    outs, refs = refs[7 : 7 + count], refs[7 + count :]
    rows_ref, picked, hidden, gate_ref, up_ref, down_ref, sems = refs
    tokens = blocks[0].shape[0]
    width, hid = gate_ref.shape
    wides, hids = spans(width, width // BLOCKS), spans(hid, HIDS)

    def streams(at, step):
        return [
            pltpu.make_async_copy(source.at[:, at], target.at[:, at], sems.at[2 * step + i])
            for i, (source, target) in enumerate(((gate_hbm, gate_ref), (up_hbm, up_ref)))
        ]

    for step, at in enumerate(hids):
        for copy in streams(at, step):
            copy.start()
    lasts = [
        pltpu.make_async_copy(down_hbm.at[:, at], down_ref.at[:, at], sems.at[2 * len(hids) + i])
        for i, at in enumerate(wides)
    ]
    for copy in lasts:
        copy.start()

    for i, ref in enumerate(blocks):
        rows_ref[i * tokens : (i + 1) * tokens] = ref[...]
    total = 0.0
    for at in wides:
        block = jnp.dot(pick_ref[...], rows_ref[:, at], preferred_element_type=jnp.float32)
        picked[:, at] = block.astype(jnp.bfloat16)
        total += jnp.sum(block * block, axis=1, keepdims=True)
    scale = lax.rsqrt(total / width + 1e-06)
    for at in wides:
        block = picked[:, at].astype(jnp.float32) * scale * gain_ref[:, at]
        picked[:, at] = block.astype(jnp.bfloat16)

    def project(step, carry):
        at = pl.ds(pl.multiple_of(step * HIDS, HIDS), HIDS)
        for copy in streams(at, step):
            copy.wait()
        first = jnp.dot(picked[...], gate_ref[:, at], preferred_element_type=jnp.float32)
        second = jnp.dot(picked[...], up_ref[:, at], preferred_element_type=jnp.float32)
        hidden[:, at] = (first / (1.0 + jnp.exp(-first)) * second).astype(jnp.bfloat16)
        return carry

    lax.fori_loop(0, len(hids), project, 0)
    for at, copy in zip(wides, lasts):
        copy.wait()
        block = jnp.dot(hidden[...], down_ref[:, at], preferred_element_type=jnp.float32)
        block = jnp.dot(put_ref[...], block.astype(jnp.bfloat16), preferred_element_type=jnp.float32)
        block = (block * weight_ref[...]).astype(jnp.bfloat16)
        for i, ref in enumerate(outs):
            ref[:, at] = block[i * tokens : (i + 1) * tokens]


def expert_call(blocks, pick, put, weight, gain, gate_cols, up_cols, down_rows):
    count, (tokens, width) = len(blocks), blocks[0].shape
    slots, hid = pick.shape[0], gate_cols.shape[1]
    whole = pl.BlockSpec(memory_space=pltpu.VMEM)
    return pl.pallas_call(
        functools.partial(expert_kernel, count),
        out_shape=[jax.ShapeDtypeStruct((tokens, width), jnp.bfloat16)] * count,
        in_specs=[whole] * (count + 4) + [pl.BlockSpec(memory_space=pltpu.HBM)] * 3,
        out_specs=[whole] * count,
        scratch_shapes=[
            pltpu.VMEM((count * tokens, width), jnp.bfloat16),
            pltpu.VMEM((slots, width), jnp.bfloat16),
            pltpu.VMEM((slots, hid), jnp.bfloat16),
            pltpu.VMEM((width, hid), jnp.bfloat16),
            pltpu.VMEM((width, hid), jnp.bfloat16),
            pltpu.VMEM((hid, width), jnp.bfloat16),
            pltpu.SemaphoreType.DMA((2 * (hid // HIDS) + BLOCKS,)),
        ],
        compiler_params=pltpu.CompilerParams(vmem_limit_bytes=(24 + count * tokens // 64) * 2**20),
        cost_estimate=pl.CostEstimate(
            flops=6 * slots * width * hid, bytes_accessed=6 * width * hid, transcendentals=slots * hid
        ),
    )(*blocks, pick, put, weight, gain, *(
        pltpu.with_memory_space_constraint(w, pltpu.HBM) for w in (gate_cols, up_cols, down_rows)
    ))


def after(values, earlier):
    return lax.optimization_barrier((values, earlier))


def on_device(
    tokens_up, tokens_down, norm_gain, w_gate, w_up, w_down, route_up, route_down, gate_up, gate_down
):
    plane, me = lax.axis_index("pipe"), lax.axis_index("expert")
    planes, experts = lax.axis_size("pipe"), lax.axis_size("expert")
    micros, tokens, width = tokens_up.shape
    top = route_up.shape[3]
    capacity = min(tokens, 2 * tokens * top // experts)
    low = plane < planes // 2
    layer = (norm_gain, w_gate[0], w_up[0], w_down[0])
    masks = list(range(0, experts, 2)) + list(range(1, experts, 2))
    half = experts // 2

    def exchange(block, mask):
        return lax.ppermute(block, "expert", [(i, i ^ mask) for i in range(experts)])

    def on_chip(outs):
        total = [
            a.astype(jnp.float32) + exchange(b, 1).astype(jnp.float32)
            for a, b in zip(outs[:half], outs[half:])
        ]
        return total[:1] + [part.astype(jnp.bfloat16) for part in total[1:]]

    def send_back(sums):
        return sums[:1] + [exchange(sums[j], masks[j]) for j in range(1, half)]

    def ordered(up, down):
        return [jnp.where(low, up, down), jnp.where(low, down, up)]

    tables = jnp.stack(
        [
            jnp.stack(ordered(route_up[0].astype(jnp.float32), route_down[0].astype(jnp.float32))),
            jnp.stack(ordered(gate_up[0], gate_down[0])),
        ]
    )
    pair = jnp.stack([tables, exchange(tables, 1)])
    tables = jnp.stack([pair] + [exchange(pair, mask) for mask in masks[1:half]], axis=1)
    tables = tables.reshape(experts, *pair.shape[1:])
    hits = (tables[:, 0] == me.astype(jnp.float32)).astype(jnp.float32)
    weights = jnp.sum(hits * tables[:, 1], axis=-1)
    hits = jnp.sum(hits, axis=-1)
    before = (jnp.arange(tokens)[:, None] < jnp.arange(tokens)[None, :]).astype(jnp.float32)
    places = jnp.einsum("dsmt,tu->dsmu", hits, before)
    places += capacity * jnp.arange(experts, dtype=jnp.float32)[:, None, None, None]
    places = jnp.where(hits > 0, places, -1.0)
    places = places.transpose(1, 2, 0, 3).reshape(2, micros, experts * tokens)
    weights = weights.transpose(1, 2, 0, 3).reshape(2, micros, experts * tokens, 1)
    slots = jnp.arange(experts * capacity, dtype=jnp.float32)
    pick = (places[:, :, None, :] == slots[:, None]).astype(jnp.bfloat16)
    put = (places[:, :, :, None] == slots).astype(jnp.bfloat16)

    entering = [jnp.where(low, tokens_up[m], tokens_down[m]) for m in range(micros)]
    results = []
    for tick in range(planes):
        stream = 0 if tick < planes // 2 else 1
        near, sums, back = [], [], []
        for m in range(micros):
            own = entering[m]
            if m > 0:
                own, near[m - 1] = after(own, near[m - 1])
            arrived = [exchange(own, mask) for mask in masks[1:half]]
            if m > 0:
                arrived, outs = after(arrived, outs)
                sums.append(on_chip(outs))
                arrived, sums[m - 1] = after(arrived, sums[m - 1])
                back.append(send_back(sums[m - 1]))
            near.append([entering[m]] + arrived)
            far = [exchange(block, 1) for block in near[m]]
            outs = expert_call(
                near[m] + far, pick[stream, m], put[stream, m], weights[stream, m], *layer
            )
            if m > 0:
                back[m - 1], outs = after(back[m - 1], outs)
        sums.append(on_chip(outs))
        back.append(send_back(sums[-1]))
        leaving = []
        for m in range(micros):
            total = entering[m].astype(jnp.float32)
            for part in back[m]:
                total += part.astype(jnp.float32)
            leaving.append(total.astype(jnp.bfloat16))
        results.append(leaving)
        if tick + 1 < planes:
            ups = [(p, p + 1) for p in range(tick % 2, planes - 1, 2)]
            pairs = ups + [(b, a) for a, b in ups]
            entering = [lax.ppermute(block, "pipe", pairs) for block in leaving]

    first = jnp.minimum(plane, planes - 1 - plane)
    acts = []
    for ticks, at in (
        (range(planes // 2), first),
        (range(planes // 2, planes), planes - 1 - first),
    ):
        chosen = jnp.stack(results[ticks[0]])
        for tick in ticks[1:]:
            chosen = jnp.where(at == tick, jnp.stack(results[tick]), chosen)
        acts.append(chosen)
    return (jnp.where(low, acts[0], acts[1])[None], jnp.where(low, acts[1], acts[0])[None])


def solution(mesh):
    in_specs = (
        P(None, "expert", None),
        P(None, "expert", None),
        P("pipe", None),
        P("pipe", None, "expert"),
        P("pipe", None, "expert"),
        P("pipe", "expert", None),
        P("pipe", None, "expert", None),
        P("pipe", None, "expert", None),
        P("pipe", None, "expert", None),
        P("pipe", None, "expert", None),
    )
    out_specs = (P("pipe", None, "expert", None), P("pipe", None, "expert", None))
    return jax.shard_map(
        on_device, mesh=mesh, in_specs=in_specs, out_specs=out_specs, check_vma=False
    )
```

profile of v0, /device:TPU:0, one launch (start us, length us, event | category | flops | bytes accessed | tf_op | source)
XLA Modules:
  0.0 247.8 jit_solution(18297849699815749081)
XLA Ops:
  3.3 2.6 %collective-permute-start = (bf16[32,3584]{1,0:T(8,128)(2,1)S(1)}, bf16[32,3584]{1,0:T(8,128)(2,1)S(1)}, u32[]{:S(2)}, u32[]{:S(2)}) collective-permute-start(bf16[32,3584]{1,0:T(8,128)(2,1)S(1)} %get-tuple-element.382.refs_0_), channel_id=1, source_target_pairs={{0,2},{1,3},{2,0},{3,1},{4,6},{5,7},{6,4},{7,5},{8,10},{9,11},{10,... | collective-permute-start | bytes 688136 | tf_op jit(solution)/shard_map/ppermute | solution.py:119
  5.8 1.5 collective-permute-start.1
  7.5 2.0 collective-permute-start.12
  9.4 1.5 collective-permute-start.11
  10.9 3.0 %collective-permute-done.13 = f32[2,2,2,2,32,2]{4,5,3,2,1,0:T(2,128)S(1)} collective-permute-done((f32[2,2,2,2,32,2]{4,5,3,2,1,0:T(2,128)S(1)}, f32[2,2,2,2,32,2]{4,5,3,2,1,0:T(2,128)S(1)}, u32[]{:S(2)}, u32[]{:S(2)}) %collective-permute-start.13) | collective-permute-done | bytes 4128 | tf_op jit(solution)/shard_map/ppermute | solution.py:119
  13.9 1.4 collective-permute-start.2
  16.9 4.6 %collective-permute-done.2.refs_3_ = bf16[32,3584]{1,0:T(8,128)(2,1)S(1)} collective-permute-done((bf16[32,3584]{1,0:T(8,128)(2,1)S(1)}, bf16[32,3584]{1,0:T(8,128)(2,1)S(1)}, u32[]{:S(2)}, u32[]{:S(2)}) %collective-permute-start.2) | collective-permute-done | bytes 229408 | tf_op jit(solution)/shard_map/ppermute | solution.py:119
  21.5 1.6 collective-permute-start.3
  23.6 1.5 collective-permute-start.5
  25.8 8.6 %shard_map.113 = (bf16[32,3584]{1,0:T(8,128)(2,1)S(1)}, bf16[32,3584]{1,0:T(8,128)(2,1)S(1)}, bf16[32,3584]{1,0:T(8,128)(2,1)S(1)}, bf16[32,3584]{1,0:T(8,128)(2...) custom-call(bf16[32,3584]{1,0:T(8,128)(2,1)S(1)} %get-tuple-element., ...), custom_call_target="tpu_custom_call" | custom-call | flops 2818572288 | bytes 22020096 | tf_op jit(solution)/shard_map/pallas_call | solution.py:78
  34.4 1.3 collective-permute-done.4.refs_2_
  42.7 1.8 collective-permute-start.20
  44.5 8.6 %shard_map.114 = (bf16[32,3584]{1,0:T(8,128)(2,1)S(1)}, bf16[32,3584]{1,0:T(8,128)(2,1)S(1)}, bf16[32,3584]{1,0:T(8,128)(2,1)S(1)}, bf16[32,3584]{1,0:T(8,128)(2...) custom-call(bf16[32,3584]{1,0:T(8,128)(2,1)S(1)} %get-tuple-element., ...), custom_call_target="tpu_custom_call" | custom-call | flops 2818572288 | bytes 22020096 | tf_op jit(solution)/shard_map/pallas_call | solution.py:78
  55.4 1.6 collective-permute-start.25
  57.1 1.5 collective-permute-start.32
  58.7 1.6 collective-permute-start.30
  60.9 2.1 collective-permute-done.25.refs_0_
  63.0 1.5 collective-permute-start.34
  65.0 1.6 collective-permute-done.32
  66.6 1.4 collective-permute-start.36
  68.0 2.2 collective-permute-done.30
  71.9 4.2 %collective-permute-done.34.refs_1_ = bf16[32,3584]{1,0:T(8,128)(2,1)S(1)} collective-permute-done((bf16[32,3584]{1,0:T(8,128)(2,1)S(1)}, bf16[32,3584]{1,0:T(8,128)(2,1)S(1)}, u32[]{:S(2)}, u32[]{:S(2)}) %collective-permute-start.34) | collective-permute-done | bytes 229408 | tf_op jit(solution)/shard_map/ppermute | solution.py:119
  76.7 3.4 %collective-permute-done.36.refs_3_ = bf16[32,3584]{1,0:T(8,128)(2,1)S(1)} collective-permute-done((bf16[32,3584]{1,0:T(8,128)(2,1)S(1)}, bf16[32,3584]{1,0:T(8,128)(2,1)S(1)}, u32[]{:S(2)}, u32[]{:S(2)}) %collective-permute-start.36) | collective-permute-done | bytes 229408 | tf_op jit(solution)/shard_map/ppermute | solution.py:119
  80.1 1.5 collective-permute-start.37
  82.1 1.5 collective-permute-start.39
  83.6 8.6 %shard_map.115 = (bf16[32,3584]{1,0:T(8,128)(2,1)S(1)}, bf16[32,3584]{1,0:T(8,128)(2,1)S(1)}, bf16[32,3584]{1,0:T(8,128)(2,1)S(1)}, bf16[32,3584]{1,0:T(8,128)(2...) custom-call(bf16[32,3584]{1,0:T(8,128)(2,1)S(1)} %collective-permute, ...), custom_call_target="tpu_custom_call" | custom-call | flops 2818572288 | bytes 22020096 | tf_op jit(solution)/shard_map/pallas_call | solution.py:78
  92.2 2.0 collective-permute-done.38.refs_2_
  99.6 1.8 collective-permute-start.50
  101.4 8.6 %shard_map.116 = (bf16[32,3584]{1,0:T(8,128)(2,1)S(1)}, bf16[32,3584]{1,0:T(8,128)(2,1)S(1)}, bf16[32,3584]{1,0:T(8,128)(2,1)S(1)}, bf16[32,3584]{1,0:T(8,128)(2...) custom-call(bf16[32,3584]{1,0:T(8,128)(2,1)S(1)} %collective-permute, ...), custom_call_target="tpu_custom_call" | custom-call | flops 2818572288 | bytes 22020096 | tf_op jit(solution)/shard_map/pallas_call | solution.py:78
  112.8 1.5 collective-permute-start.61
  114.4 1.6 collective-permute-start.59
  116.6 1.5 collective-permute-start.64
  118.6 3.6 %collective-permute-done.61 = bf16[32,3584]{1,0:T(8,128)(2,1)S(1)} collective-permute-done((bf16[32,3584]{1,0:T(8,128)(2,1)S(1)}, bf16[32,3584]{1,0:T(8,128)(2,1)S(1)}, u32[]{:S(2)}, u32[]{:S(2)}) %collective-permute-start.61) | collective-permute-done | bytes 229408 | tf_op jit(solution)/shard_map/ppermute | solution.py:119
  122.3 1.4 collective-permute-start.66
  123.7 2.6 %collective-permute-done.59 = bf16[32,3584]{1,0:T(8,128)(2,1)S(1)} collective-permute-done((bf16[32,3584]{1,0:T(8,128)(2,1)S(1)}, bf16[32,3584]{1,0:T(8,128)(2,1)S(1)}, u32[]{:S(2)}, u32[]{:S(2)}) %collective-permute-start.59) | collective-permute-done | bytes 229408 | tf_op jit(solution)/shard_map/ppermute | solution.py:119
  127.9 4.0 %collective-permute-done.64.refs_1_ = bf16[32,3584]{1,0:T(8,128)(2,1)S(1)} collective-permute-done((bf16[32,3584]{1,0:T(8,128)(2,1)S(1)}, bf16[32,3584]{1,0:T(8,128)(2,1)S(1)}, u32[]{:S(2)}, u32[]{:S(2)}) %collective-permute-start.64) | collective-permute-done | bytes 229408 | tf_op jit(solution)/shard_map/ppermute | solution.py:119
  132.4 3.7 %collective-permute-done.66.refs_3_ = bf16[32,3584]{1,0:T(8,128)(2,1)S(1)} collective-permute-done((bf16[32,3584]{1,0:T(8,128)(2,1)S(1)}, bf16[32,3584]{1,0:T(8,128)(2,1)S(1)}, u32[]{:S(2)}, u32[]{:S(2)}) %collective-permute-start.66) | collective-permute-done | bytes 229408 | tf_op jit(solution)/shard_map/ppermute | solution.py:119
  136.2 1.6 collective-permute-start.67
  138.3 1.5 collective-permute-start.69
  139.8 8.6 %shard_map.117 = (bf16[32,3584]{1,0:T(8,128)(2,1)S(1)}, bf16[32,3584]{1,0:T(8,128)(2,1)S(1)}, bf16[32,3584]{1,0:T(8,128)(2,1)S(1)}, bf16[32,3584]{1,0:T(8,128)(2...) custom-call(bf16[32,3584]{1,0:T(8,128)(2,1)S(1)} %collective-permute, ...), custom_call_target="tpu_custom_call" | custom-call | flops 2818572288 | bytes 22020096 | tf_op jit(solution)/shard_map/pallas_call | solution.py:78
  148.4 2.0 collective-permute-done.68.refs_2_
  157.0 1.8 collective-permute-start.80
  158.8 8.6 %shard_map.118 = (bf16[32,3584]{1,0:T(8,128)(2,1)S(1)}, bf16[32,3584]{1,0:T(8,128)(2,1)S(1)}, bf16[32,3584]{1,0:T(8,128)(2,1)S(1)}, bf16[32,3584]{1,0:T(8,128)(2...) custom-call(bf16[32,3584]{1,0:T(8,128)(2,1)S(1)} %collective-permute, ...), custom_call_target="tpu_custom_call" | custom-call | flops 2818572288 | bytes 22020096 | tf_op jit(solution)/shard_map/pallas_call | solution.py:78
  169.7 4.2 %collective-permute-start.85 = (bf16[32,3584]{1,0:T(8,128)(2,1)S(1)}, bf16[32,3584]{1,0:T(8,128)(2,1)S(1)}, u32[]{:S(2)}, u32[]{:S(2)}) collective-permute-start(bf16[32,3584]{1,0:T(8,128)(2,1)S(1)} %add_convert_fusion.12), channel_id=1, source_target_pairs={{0,8},{16,24},{8,0},{24,16},{1,9},{17,25},{9,1},{25,17},{2,10},{18... | collective-permute-start | bytes 688136 | tf_op jit(solution)/shard_map/ppermute | solution.py:190
  173.9 1.5 collective-permute-start.92
  175.5 1.6 collective-permute-start.90
  177.7 1.9 collective-permute-done.85.refs_0_
  179.6 1.5 collective-permute-start.94
  181.6 1.8 collective-permute-done.92
  183.4 1.4 collective-permute-start.96
  184.9 2.2 collective-permute-done.90
  188.5 4.5 %collective-permute-done.94.refs_1_ = bf16[32,3584]{1,0:T(8,128)(2,1)S(1)} collective-permute-done((bf16[32,3584]{1,0:T(8,128)(2,1)S(1)}, bf16[32,3584]{1,0:T(8,128)(2,1)S(1)}, u32[]{:S(2)}, u32[]{:S(2)}) %collective-permute-start.94) | collective-permute-done | bytes 229408 | tf_op jit(solution)/shard_map/ppermute | solution.py:119
  193.5 3.4 %collective-permute-done.96.refs_3_ = bf16[32,3584]{1,0:T(8,128)(2,1)S(1)} collective-permute-done((bf16[32,3584]{1,0:T(8,128)(2,1)S(1)}, bf16[32,3584]{1,0:T(8,128)(2,1)S(1)}, u32[]{:S(2)}, u32[]{:S(2)}) %collective-permute-start.96) | collective-permute-done | bytes 229408 | tf_op jit(solution)/shard_map/ppermute | solution.py:119
  196.9 1.5 collective-permute-start.97
  198.9 1.5 collective-permute-start.99
  200.4 8.6 %shard_map.119 = (bf16[32,3584]{1,0:T(8,128)(2,1)S(1)}, bf16[32,3584]{1,0:T(8,128)(2,1)S(1)}, bf16[32,3584]{1,0:T(8,128)(2,1)S(1)}, bf16[32,3584]{1,0:T(8,128)(2...) custom-call(bf16[32,3584]{1,0:T(8,128)(2,1)S(1)} %collective-permute, ...), custom_call_target="tpu_custom_call" | custom-call | flops 2818572288 | bytes 22020096 | tf_op jit(solution)/shard_map/pallas_call | solution.py:78
  209.0 2.0 collective-permute-done.98.refs_2_
  216.4 1.8 collective-permute-start.110
  218.2 8.6 %shard_map.120 = (bf16[32,3584]{1,0:T(8,128)(2,1)S(1)}, bf16[32,3584]{1,0:T(8,128)(2,1)S(1)}, bf16[32,3584]{1,0:T(8,128)(2,1)S(1)}, bf16[32,3584]{1,0:T(8,128)(2...) custom-call(bf16[32,3584]{1,0:T(8,128)(2,1)S(1)} %collective-permute, ...), custom_call_target="tpu_custom_call" | custom-call | flops 2818572288 | bytes 22020096 | tf_op jit(solution)/shard_map/pallas_call | solution.py:78
  231.4 1.5 collective-permute-start.121
  232.9 1.6 collective-permute-start.119
  236.5 4.3 %collective-permute-done.121 = bf16[32,3584]{1,0:T(8,128)(2,1)S(1)} collective-permute-done((bf16[32,3584]{1,0:T(8,128)(2,1)S(1)}, bf16[32,3584]{1,0:T(8,128)(2,1)S(1)}, u32[]{:S(2)}, u32[]{:S(2)}) %collective-permute-start.121) | collective-permute-done | bytes 229408 | tf_op jit(solution)/shard_map/ppermute | solution.py:119
  240.8 4.1 %collective-permute-done.119 = bf16[32,3584]{1,0:T(8,128)(2,1)S(1)} collective-permute-done((bf16[32,3584]{1,0:T(8,128)(2,1)S(1)}, bf16[32,3584]{1,0:T(8,128)(2,1)S(1)}, u32[]{:S(2)}, u32[]{:S(2)}) %collective-permute-start.119) | collective-permute-done | bytes 229408 | tf_op jit(solution)/shard_map/ppermute | solution.py:119
  245.1 2.4 broadcast_select_fusion
  (267 shorter events, 55.6 us)
Async XLA Ops:
  3.3 13.0 %collective-permute-start = (bf16[32,3584]{1,0:T(8,128)(2,1)S(1)}, bf16[32,3584]{1,0:T(8,128)(2,1)S(1)}, u32[]{:S(2)}, u32[]{:S(2)}) collective-permute-start(bf16[32,3584]{1,0:T(8,128)(2,1)S(1)} %get-tuple-element.382.refs_0_), channel_id=1, source_target_pairs={{0,2},{1,3},{2,0},{3,1},{4,6},{5,7},{6,4},{7,5},{8,10},{9,11},{10,... | collective-permute-start | bytes 688136 | tf_op jit(solution)/shard_map/ppermute | solution.py:119
  5.8 11.0 %collective-permute-start.1 = (bf16[32,3584]{1,0:T(8,128)(2,1)S(1)}, bf16[32,3584]{1,0:T(8,128)(2,1)S(1)}, u32[]{:S(2)}, u32[]{:S(2)}) collective-permute-start(bf16[32,3584]{1,0:T(8,128)(2,1)S(1)} %get-tuple-element.382.refs_0_), channel_id=1, source_target_pairs={{0,4},{1,5},{2,6},{3,7},{4,0},{5,1},{6,2},{7,3},{8,12},{9,13},{10,... | collective-permute-start | bytes 688136 | tf_op jit(solution)/shard_map/ppermute | solution.py:119
  7.5 7.9 %collective-permute-start.12 = (f32[2,2,2,2,32,2]{4,5,3,2,1,0:T(2,128)S(1)}, f32[2,2,2,2,32,2]{4,5,3,2,1,0:T(2,128)S(1)}, u32[]{:S(2)}, u32[]{:S(2)}) collective-permute-start(f32[2,2,2,2,32,2]{4,5,3,2,1,0:T(2,128)S(1)} %get-tuple-element.393), channel_id=1, source_target_pairs={{0,4},{1,5},{2,6},{3,7},{4,0},{5,1},{6,2},{7,3},{8,12},{9,13},{10,... | collective-permute-start | bytes 12296 | tf_op jit(solution)/shard_map/ppermute | solution.py:119
  13.9 7.5 %collective-permute-start.2 = (bf16[32,3584]{1,0:T(8,128)(2,1)S(1)}, bf16[32,3584]{1,0:T(8,128)(2,1)S(1)}, u32[]{:S(2)}, u32[]{:S(2)}) collective-permute-start(bf16[32,3584]{1,0:T(8,128)(2,1)S(1)} %get-tuple-element.382.refs_0_), channel_id=1, source_target_pairs={{0,6},{1,7},{2,4},{3,5},{4,2},{5,3},{6,0},{7,1},{8,14},{9,15},{10,... | collective-permute-start | bytes 688136 | tf_op jit(solution)/shard_map/ppermute | solution.py:119
  15.4 7.7 %collective-permute-start.6 = (bf16[32,3584]{1,0:T(8,128)(2,1)S(1)}, bf16[32,3584]{1,0:T(8,128)(2,1)S(1)}, u32[]{:S(2)}, u32[]{:S(2)}) collective-permute-start(bf16[32,3584]{1,0:T(8,128)(2,1)S(1)} %get-tuple-element.382.refs_0_), channel_id=1, source_target_pairs={{0,1},{1,0},{2,3},{3,2},{4,5},{5,4},{6,7},{7,6},{8,9},{9,8},{10,11... | collective-permute-start | bytes 688136 | tf_op jit(solution)/shard_map/ppermute | solution.py:119
  16.8 8.2 %collective-permute-start.8 = (bf16[32,3584]{1,0:T(8,128)(2,1)S(1)}, bf16[32,3584]{1,0:T(8,128)(2,1)S(1)}, u32[]{:S(2)}, u32[]{:S(2)}) collective-permute-start(bf16[32,3584]{1,0:T(8,128)(2,1)S(1)} %collective-permute-done.1.refs_2_), channel_id=1, source_target_pairs={{0,1},{1,0},{2,3},{3,2},{4,5},{5,4},{6,7},{7,6},{8,9},{9,8},{10,11... | collective-permute-start | bytes 688136 | tf_op jit(solution)/shard_map/ppermute | solution.py:119
  21.5 12.9 %collective-permute-start.3 = (bf16[32,3584]{1,0:T(8,128)(2,1)S(1)}, bf16[32,3584]{1,0:T(8,128)(2,1)S(1)}, u32[]{:S(2)}, u32[]{:S(2)}) collective-permute-start(bf16[32,3584]{1,0:T(8,128)(2,1)S(1)} %get-tuple-element.190.refs_0_), channel_id=1, source_target_pairs={{0,2},{1,3},{2,0},{3,1},{4,6},{5,7},{6,4},{7,5},{8,10},{9,11},{10,... | collective-permute-start | bytes 688136 | tf_op jit(solution)/shard_map/ppermute | solution.py:119
  23.1 12.7 %collective-permute-start.4 = (bf16[32,3584]{1,0:T(8,128)(2,1)S(1)}, bf16[32,3584]{1,0:T(8,128)(2,1)S(1)}, u32[]{:S(2)}, u32[]{:S(2)}) collective-permute-start(bf16[32,3584]{1,0:T(8,128)(2,1)S(1)} %get-tuple-element.190.refs_0_), channel_id=1, source_target_pairs={{0,4},{1,5},{2,6},{3,7},{4,0},{5,1},{6,2},{7,3},{8,12},{9,13},{10,... | collective-permute-start | bytes 688136 | tf_op jit(solution)/shard_map/ppermute | solution.py:119
  23.6 12.1 %collective-permute-start.5 = (bf16[32,3584]{1,0:T(8,128)(2,1)S(1)}, bf16[32,3584]{1,0:T(8,128)(2,1)S(1)}, u32[]{:S(2)}, u32[]{:S(2)}) collective-permute-start(bf16[32,3584]{1,0:T(8,128)(2,1)S(1)} %get-tuple-element.190.refs_0_), channel_id=1, source_target_pairs={{0,6},{1,7},{2,4},{3,5},{4,2},{5,3},{6,0},{7,1},{8,14},{9,15},{10,... | collective-permute-start | bytes 688136 | tf_op jit(solution)/shard_map/ppermute | solution.py:119
  40.9 12.2 %collective-permute-start.18 = (bf16[32,3584]{1,0:T(8,128)(2,1)}, bf16[32,3584]{1,0:T(8,128)(2,1)S(1)}, u32[]{:S(2)}, u32[]{:S(2)}) collective-permute-start(bf16[32,3584]{1,0:T(8,128)(2,1)} %add_convert_fusion.31), channel_id=1, source_target_pairs={{0,2},{1,3},{2,0},{3,1},{4,6},{5,7},{6,4},{7,5},{8,10},{9,11},{10,... | collective-permute-start | bytes 688136 | tf_op jit(solution)/shard_map/ppermute | solution.py:119
  41.5 12.7 %collective-permute-start.19 = (bf16[32,3584]{1,0:T(8,128)(2,1)}, bf16[32,3584]{1,0:T(8,128)(2,1)S(1)}, u32[]{:S(2)}, u32[]{:S(2)}) collective-permute-start(bf16[32,3584]{1,0:T(8,128)(2,1)} %add_convert_fusion.30), channel_id=1, source_target_pairs={{0,4},{1,5},{2,6},{3,7},{4,0},{5,1},{6,2},{7,3},{8,12},{9,13},{10,... | collective-permute-start | bytes 688136 | tf_op jit(solution)/shard_map/ppermute | solution.py:119
  42.7 11.5 %collective-permute-start.20 = (bf16[32,3584]{1,0:T(8,128)(2,1)}, bf16[32,3584]{1,0:T(8,128)(2,1)S(1)}, u32[]{:S(2)}, u32[]{:S(2)}) collective-permute-start(bf16[32,3584]{1,0:T(8,128)(2,1)} %add_convert_fusion.29), channel_id=1, source_target_pairs={{0,6},{1,7},{2,4},{3,5},{4,2},{5,3},{6,0},{7,1},{8,14},{9,15},{10,... | collective-permute-start | bytes 688136 | tf_op jit(solution)/shard_map/ppermute | solution.py:119
  54.7 9.7 %collective-permute-start.26 = (bf16[32,3584]{1,0:T(8,128)(2,1)S(1)}, bf16[32,3584]{1,0:T(8,128)(2,1)S(1)}, u32[]{:S(2)}, u32[]{:S(2)}) collective-permute-start(bf16[32,3584]{1,0:T(8,128)(2,1)S(1)} %get-tuple-element.230), channel_id=1, source_target_pairs={{0,1},{1,0},{2,3},{3,2},{4,5},{5,4},{6,7},{7,6},{8,9},{9,8},{10,11... | collective-permute-start | bytes 688136 | tf_op jit(solution)/shard_map/ppermute | solution.py:119
  55.4 7.6 %collective-permute-start.25 = (bf16[32,3584]{1,0:T(8,128)(2,1)S(1)}, bf16[32,3584]{1,0:T(8,128)(2,1)S(1)}, u32[]{:S(2)}, u32[]{:S(2)}) collective-permute-start(bf16[32,3584]{1,0:T(8,128)(2,1)S(1)} %add_convert_fusion.28), channel_id=1, source_target_pairs={{0,8},{16,24},{8,0},{24,16},{1,9},{17,25},{9,1},{25,17},{2,10},{18... | collective-permute-start | bytes 688136 | tf_op jit(solution)/shard_map/ppermute | solution.py:190
  57.1 9.5 %collective-permute-start.32 = (bf16[32,3584]{1,0:T(8,128)(2,1)S(1)}, bf16[32,3584]{1,0:T(8,128)(2,1)S(1)}, u32[]{:S(2)}, u32[]{:S(2)}) collective-permute-start(bf16[32,3584]{1,0:T(8,128)(2,1)S(1)} %add_convert_fusion.25), channel_id=1, source_target_pairs={{0,6},{1,7},{2,4},{3,5},{4,2},{5,3},{6,0},{7,1},{8,14},{9,15},{10,... | collective-permute-start | bytes 688136 | tf_op jit(solution)/shard_map/ppermute | solution.py:119
  58.7 11.6 %collective-permute-start.30 = (bf16[32,3584]{1,0:T(8,128)(2,1)S(1)}, bf16[32,3584]{1,0:T(8,128)(2,1)S(1)}, u32[]{:S(2)}, u32[]{:S(2)}) collective-permute-start(bf16[32,3584]{1,0:T(8,128)(2,1)S(1)} %add_convert_fusion.26), channel_id=1, source_target_pairs={{0,4},{1,5},{2,6},{3,7},{4,0},{5,1},{6,2},{7,3},{8,12},{9,13},{10,... | collective-permute-start | bytes 688136 | tf_op jit(solution)/shard_map/ppermute | solution.py:119
  60.3 11.0 %collective-permute-start.28 = (bf16[32,3584]{1,0:T(8,128)(2,1)S(1)}, bf16[32,3584]{1,0:T(8,128)(2,1)S(1)}, u32[]{:S(2)}, u32[]{:S(2)}) collective-permute-start(bf16[32,3584]{1,0:T(8,128)(2,1)S(1)} %add_convert_fusion.27), channel_id=1, source_target_pairs={{0,2},{1,3},{2,0},{3,1},{4,6},{5,7},{6,4},{7,5},{8,10},{9,11},{10,... | collective-permute-start | bytes 688136 | tf_op jit(solution)/shard_map/ppermute | solution.py:119
  63.0 13.2 %collective-permute-start.34 = (bf16[32,3584]{1,0:T(8,128)(2,1)S(1)}, bf16[32,3584]{1,0:T(8,128)(2,1)S(1)}, u32[]{:S(2)}, u32[]{:S(2)}) collective-permute-start(bf16[32,3584]{1,0:T(8,128)(2,1)S(1)} %collective-permute-done.25.refs_0_), channel_id=1, source_target_pairs={{0,2},{1,3},{2,0},{3,1},{4,6},{5,7},{6,4},{7,5},{8,10},{9,11},{10,... | collective-permute-start | bytes 688136 | tf_op jit(solution)/shard_map/ppermute | solution.py:119
  64.5 11.9 %collective-permute-start.35 = (bf16[32,3584]{1,0:T(8,128)(2,1)S(1)}, bf16[32,3584]{1,0:T(8,128)(2,1)S(1)}, u32[]{:S(2)}, u32[]{:S(2)}) collective-permute-start(bf16[32,3584]{1,0:T(8,128)(2,1)S(1)} %collective-permute-done.25.refs_0_), channel_id=1, source_target_pairs={{0,4},{1,5},{2,6},{3,7},{4,0},{5,1},{6,2},{7,3},{8,12},{9,13},{10,... | collective-permute-start | bytes 688136 | tf_op jit(solution)/shard_map/ppermute | solution.py:119
  66.6 13.5 %collective-permute-start.36 = (bf16[32,3584]{1,0:T(8,128)(2,1)S(1)}, bf16[32,3584]{1,0:T(8,128)(2,1)S(1)}, u32[]{:S(2)}, u32[]{:S(2)}) collective-permute-start(bf16[32,3584]{1,0:T(8,128)(2,1)S(1)} %collective-permute-done.25.refs_0_), channel_id=1, source_target_pairs={{0,6},{1,7},{2,4},{3,5},{4,2},{5,3},{6,0},{7,1},{8,14},{9,15},{10,... | collective-permute-start | bytes 688136 | tf_op jit(solution)/shard_map/ppermute | solution.py:119
  71.4 8.6 %collective-permute-start.33 = (bf16[32,3584]{1,0:T(8,128)(2,1)S(1)}, bf16[32,3584]{1,0:T(8,128)(2,1)S(1)}, u32[]{:S(2)}, u32[]{:S(2)}) collective-permute-start(bf16[32,3584]{1,0:T(8,128)(2,1)S(1)} %add_convert_fusion.24), channel_id=1, source_target_pairs={{0,8},{16,24},{8,0},{24,16},{1,9},{17,25},{9,1},{25,17},{2,10},{18... | collective-permute-start | bytes 688136 | tf_op jit(solution)/shard_map/ppermute | solution.py:190
  71.9 9.7 %collective-permute-start.40 = (bf16[32,3584]{1,0:T(8,128)(2,1)S(1)}, bf16[32,3584]{1,0:T(8,128)(2,1)S(1)}, u32[]{:S(2)}, u32[]{:S(2)}) collective-permute-start(bf16[32,3584]{1,0:T(8,128)(2,1)S(1)} %collective-permute-done.25.refs_0_), channel_id=1, source_target_pairs={{0,1},{1,0},{2,3},{3,2},{4,5},{5,4},{6,7},{7,6},{8,9},{9,8},{10,11... | collective-permute-start | bytes 688136 | tf_op jit(solution)/shard_map/ppermute | solution.py:119
  80.1 12.1 %collective-permute-start.37 = (bf16[32,3584]{1,0:T(8,128)(2,1)S(1)}, bf16[32,3584]{1,0:T(8,128)(2,1)S(1)}, u32[]{:S(2)}, u32[]{:S(2)}) collective-permute-start(bf16[32,3584]{1,0:T(8,128)(2,1)S(1)} %collective-permute-done.33.refs_0_), channel_id=1, source_target_pairs={{0,2},{1,3},{2,0},{3,1},{4,6},{5,7},{6,4},{7,5},{8,10},{9,11},{10,... | collective-permute-start | bytes 688136 | tf_op jit(solution)/shard_map/ppermute | solution.py:119
  81.6 12.7 %collective-permute-start.38 = (bf16[32,3584]{1,0:T(8,128)(2,1)S(1)}, bf16[32,3584]{1,0:T(8,128)(2,1)S(1)}, u32[]{:S(2)}, u32[]{:S(2)}) collective-permute-start(bf16[32,3584]{1,0:T(8,128)(2,1)S(1)} %collective-permute-done.33.refs_0_), channel_id=1, source_target_pairs={{0,4},{1,5},{2,6},{3,7},{4,0},{5,1},{6,2},{7,3},{8,12},{9,13},{10,... | collective-permute-start | bytes 688136 | tf_op jit(solution)/shard_map/ppermute | solution.py:119
  82.1 12.1 %collective-permute-start.39 = (bf16[32,3584]{1,0:T(8,128)(2,1)S(1)}, bf16[32,3584]{1,0:T(8,128)(2,1)S(1)}, u32[]{:S(2)}, u32[]{:S(2)}) collective-permute-start(bf16[32,3584]{1,0:T(8,128)(2,1)S(1)} %collective-permute-done.33.refs_0_), channel_id=1, source_target_pairs={{0,6},{1,7},{2,4},{3,5},{4,2},{5,3},{6,0},{7,1},{8,14},{9,15},{10,... | collective-permute-start | bytes 688136 | tf_op jit(solution)/shard_map/ppermute | solution.py:119
  97.9 12.1 %collective-permute-start.48 = (bf16[32,3584]{1,0:T(8,128)(2,1)S(1)}, bf16[32,3584]{1,0:T(8,128)(2,1)S(1)}, u32[]{:S(2)}, u32[]{:S(2)}) collective-permute-start(bf16[32,3584]{1,0:T(8,128)(2,1)S(1)} %add_convert_fusion.23), channel_id=1, source_target_pairs={{0,2},{1,3},{2,0},{3,1},{4,6},{5,7},{6,4},{7,5},{8,10},{9,11},{10,... | collective-permute-start | bytes 688136 | tf_op jit(solution)/shard_map/ppermute | solution.py:119
  98.4 12.5 %collective-permute-start.49 = (bf16[32,3584]{1,0:T(8,128)(2,1)S(1)}, bf16[32,3584]{1,0:T(8,128)(2,1)S(1)}, u32[]{:S(2)}, u32[]{:S(2)}) collective-permute-start(bf16[32,3584]{1,0:T(8,128)(2,1)S(1)} %add_convert_fusion.22), channel_id=1, source_target_pairs={{0,4},{1,5},{2,6},{3,7},{4,0},{5,1},{6,2},{7,3},{8,12},{9,13},{10,... | collective-permute-start | bytes 688136 | tf_op jit(solution)/shard_map/ppermute | solution.py:119
  99.6 11.3 %collective-permute-start.50 = (bf16[32,3584]{1,0:T(8,128)(2,1)S(1)}, bf16[32,3584]{1,0:T(8,128)(2,1)S(1)}, u32[]{:S(2)}, u32[]{:S(2)}) collective-permute-start(bf16[32,3584]{1,0:T(8,128)(2,1)S(1)} %add_convert_fusion.21), channel_id=1, source_target_pairs={{0,6},{1,7},{2,4},{3,5},{4,2},{5,3},{6,0},{7,1},{8,14},{9,15},{10,... | collective-permute-start | bytes 688136 | tf_op jit(solution)/shard_map/ppermute | solution.py:119
  112.8 9.5 %collective-permute-start.61 = (bf16[32,3584]{1,0:T(8,128)(2,1)S(1)}, bf16[32,3584]{1,0:T(8,128)(2,1)S(1)}, u32[]{:S(2)}, u32[]{:S(2)}) collective-permute-start(bf16[32,3584]{1,0:T(8,128)(2,1)S(1)} %add_convert_fusion.17), channel_id=1, source_target_pairs={{0,6},{1,7},{2,4},{3,5},{4,2},{5,3},{6,0},{7,1},{8,14},{9,15},{10,... | collective-permute-start | bytes 688136 | tf_op jit(solution)/shard_map/ppermute | solution.py:119
  114.4 11.9 %collective-permute-start.59 = (bf16[32,3584]{1,0:T(8,128)(2,1)S(1)}, bf16[32,3584]{1,0:T(8,128)(2,1)S(1)}, u32[]{:S(2)}, u32[]{:S(2)}) collective-permute-start(bf16[32,3584]{1,0:T(8,128)(2,1)S(1)} %add_convert_fusion.18), channel_id=1, source_target_pairs={{0,4},{1,5},{2,6},{3,7},{4,0},{5,1},{6,2},{7,3},{8,12},{9,13},{10,... | collective-permute-start | bytes 688136 | tf_op jit(solution)/shard_map/ppermute | solution.py:119
  116.0 10.9 %collective-permute-start.57 = (bf16[32,3584]{1,0:T(8,128)(2,1)S(1)}, bf16[32,3584]{1,0:T(8,128)(2,1)S(1)}, u32[]{:S(2)}, u32[]{:S(2)}) collective-permute-start(bf16[32,3584]{1,0:T(8,128)(2,1)S(1)} %add_convert_fusion.19), channel_id=1, source_target_pairs={{0,2},{1,3},{2,0},{3,1},{4,6},{5,7},{6,4},{7,5},{8,10},{9,11},{10,... | collective-permute-start | bytes 688136 | tf_op jit(solution)/shard_map/ppermute | solution.py:119
  116.6 15.2 %collective-permute-start.64 = (bf16[32,3584]{1,0:T(8,128)(2,1)S(1)}, bf16[32,3584]{1,0:T(8,128)(2,1)S(1)}, u32[]{:S(2)}, u32[]{:S(2)}) collective-permute-start(bf16[32,3584]{1,0:T(8,128)(2,1)S(1)} %collective-permute-done.62.refs_0_), channel_id=1, source_target_pairs={{0,2},{1,3},{2,0},{3,1},{4,6},{5,7},{6,4},{7,5},{8,10},{9,11},{10,... | collective-permute-start | bytes 688136 | tf_op jit(solution)/shard_map/ppermute | solution.py:119
  118.1 13.9 %collective-permute-start.65 = (bf16[32,3584]{1,0:T(8,128)(2,1)S(1)}, bf16[32,3584]{1,0:T(8,128)(2,1)S(1)}, u32[]{:S(2)}, u32[]{:S(2)}) collective-permute-start(bf16[32,3584]{1,0:T(8,128)(2,1)S(1)} %collective-permute-done.62.refs_0_), channel_id=1, source_target_pairs={{0,4},{1,5},{2,6},{3,7},{4,0},{5,1},{6,2},{7,3},{8,12},{9,13},{10,... | collective-permute-start | bytes 688136 | tf_op jit(solution)/shard_map/ppermute | solution.py:119
  122.3 13.8 %collective-permute-start.66 = (bf16[32,3584]{1,0:T(8,128)(2,1)S(1)}, bf16[32,3584]{1,0:T(8,128)(2,1)S(1)}, u32[]{:S(2)}, u32[]{:S(2)}) collective-permute-start(bf16[32,3584]{1,0:T(8,128)(2,1)S(1)} %collective-permute-done.62.refs_0_), channel_id=1, source_target_pairs={{0,6},{1,7},{2,4},{3,5},{4,2},{5,3},{6,0},{7,1},{8,14},{9,15},{10,... | collective-permute-start | bytes 688136 | tf_op jit(solution)/shard_map/ppermute | solution.py:119
  127.1 9.1 %collective-permute-start.63 = (bf16[32,3584]{1,0:T(8,128)(2,1)S(1)}, bf16[32,3584]{1,0:T(8,128)(2,1)S(1)}, u32[]{:S(2)}, u32[]{:S(2)}) collective-permute-start(bf16[32,3584]{1,0:T(8,128)(2,1)S(1)} %add_convert_fusion.16), channel_id=1, source_target_pairs={{8,16},{16,8},{9,17},{17,9},{10,18},{18,10},{11,19},{19,11},{12,20... | collective-permute-start | bytes 688136 | tf_op jit(solution)/shard_map/ppermute | solution.py:190
  127.8 10.0 %collective-permute-start.70 = (bf16[32,3584]{1,0:T(8,128)(2,1)S(1)}, bf16[32,3584]{1,0:T(8,128)(2,1)S(1)}, u32[]{:S(2)}, u32[]{:S(2)}) collective-permute-start(bf16[32,3584]{1,0:T(8,128)(2,1)S(1)} %collective-permute-done.62.refs_0_), channel_id=1, source_target_pairs={{0,1},{1,0},{2,3},{3,2},{4,5},{5,4},{6,7},{7,6},{8,9},{9,8},{10,11... | collective-permute-start | bytes 688136 | tf_op jit(solution)/shard_map/ppermute | solution.py:119
  132.0 7.8 %collective-permute-start.72 = (bf16[32,3584]{1,0:T(8,128)(2,1)S(1)}, bf16[32,3584]{1,0:T(8,128)(2,1)S(1)}, u32[]{:S(2)}, u32[]{:S(2)}) collective-permute-start(bf16[32,3584]{1,0:T(8,128)(2,1)S(1)} %collective-permute-done.65.refs_2_), channel_id=1, source_target_pairs={{0,1},{1,0},{2,3},{3,2},{4,5},{5,4},{6,7},{7,6},{8,9},{9,8},{10,11... | collective-permute-start | bytes 688136 | tf_op jit(solution)/shard_map/ppermute | solution.py:119
  136.2 12.2 %collective-permute-start.67 = (bf16[32,3584]{1,0:T(8,128)(2,1)S(1)}, bf16[32,3584]{1,0:T(8,128)(2,1)S(1)}, u32[]{:S(2)}, u32[]{:S(2)}) collective-permute-start(bf16[32,3584]{1,0:T(8,128)(2,1)S(1)} %collective-permute-done.63.refs_0_), channel_id=1, source_target_pairs={{0,2},{1,3},{2,0},{3,1},{4,6},{5,7},{6,4},{7,5},{8,10},{9,11},{10,... | collective-permute-start | bytes 688136 | tf_op jit(solution)/shard_map/ppermute | solution.py:119
  137.8 12.7 %collective-permute-start.68 = (bf16[32,3584]{1,0:T(8,128)(2,1)S(1)}, bf16[32,3584]{1,0:T(8,128)(2,1)S(1)}, u32[]{:S(2)}, u32[]{:S(2)}) collective-permute-start(bf16[32,3584]{1,0:T(8,128)(2,1)S(1)} %collective-permute-done.63.refs_0_), channel_id=1, source_target_pairs={{0,4},{1,5},{2,6},{3,7},{4,0},{5,1},{6,2},{7,3},{8,12},{9,13},{10,... | collective-permute-start | bytes 688136 | tf_op jit(solution)/shard_map/ppermute | solution.py:119
  138.3 12.1 %collective-permute-start.69 = (bf16[32,3584]{1,0:T(8,128)(2,1)S(1)}, bf16[32,3584]{1,0:T(8,128)(2,1)S(1)}, u32[]{:S(2)}, u32[]{:S(2)}) collective-permute-start(bf16[32,3584]{1,0:T(8,128)(2,1)S(1)} %collective-permute-done.63.refs_0_), channel_id=1, source_target_pairs={{0,6},{1,7},{2,4},{3,5},{4,2},{5,3},{6,0},{7,1},{8,14},{9,15},{10,... | collective-permute-start | bytes 688136 | tf_op jit(solution)/shard_map/ppermute | solution.py:119
  155.2 12.2 %collective-permute-start.78 = (bf16[32,3584]{1,0:T(8,128)(2,1)S(1)}, bf16[32,3584]{1,0:T(8,128)(2,1)S(1)}, u32[]{:S(2)}, u32[]{:S(2)}) collective-permute-start(bf16[32,3584]{1,0:T(8,128)(2,1)S(1)} %add_convert_fusion.15), channel_id=1, source_target_pairs={{0,2},{1,3},{2,0},{3,1},{4,6},{5,7},{6,4},{7,5},{8,10},{9,11},{10,... | collective-permute-start | bytes 688136 | tf_op jit(solution)/shard_map/ppermute | solution.py:119
  155.8 12.7 %collective-permute-start.79 = (bf16[32,3584]{1,0:T(8,128)(2,1)}, bf16[32,3584]{1,0:T(8,128)(2,1)S(1)}, u32[]{:S(2)}, u32[]{:S(2)}) collective-permute-start(bf16[32,3584]{1,0:T(8,128)(2,1)} %add_convert_fusion.14), channel_id=1, source_target_pairs={{0,4},{1,5},{2,6},{3,7},{4,0},{5,1},{6,2},{7,3},{8,12},{9,13},{10,... | collective-permute-start | bytes 688136 | tf_op jit(solution)/shard_map/ppermute | solution.py:119
  157.0 11.5 %collective-permute-start.80 = (bf16[32,3584]{1,0:T(8,128)(2,1)}, bf16[32,3584]{1,0:T(8,128)(2,1)S(1)}, u32[]{:S(2)}, u32[]{:S(2)}) collective-permute-start(bf16[32,3584]{1,0:T(8,128)(2,1)} %add_convert_fusion.13), channel_id=1, source_target_pairs={{0,6},{1,7},{2,4},{3,5},{4,2},{5,3},{6,0},{7,1},{8,14},{9,15},{10,... | collective-permute-start | bytes 688136 | tf_op jit(solution)/shard_map/ppermute | solution.py:119
  169.0 8.0 %collective-permute-start.87 = (bf16[32,3584]{1,0:T(8,128)(2,1)S(1)}, bf16[32,3584]{1,0:T(8,128)(2,1)S(1)}, u32[]{:S(2)}, u32[]{:S(2)}) collective-permute-start(bf16[32,3584]{1,0:T(8,128)(2,1)S(1)} %get-tuple-element.326), channel_id=1, source_target_pairs={{0,1},{1,0},{2,3},{3,2},{4,5},{5,4},{6,7},{7,6},{8,9},{9,8},{10,11... | collective-permute-start | bytes 688136 | tf_op jit(solution)/shard_map/ppermute | solution.py:119
  169.0 12.1 %collective-permute-start.86 = (bf16[32,3584]{1,0:T(8,128)(2,1)S(1)}, bf16[32,3584]{1,0:T(8,128)(2,1)S(1)}, u32[]{:S(2)}, u32[]{:S(2)}) collective-permute-start(bf16[32,3584]{1,0:T(8,128)(2,1)S(1)} %get-tuple-element.324), channel_id=1, source_target_pairs={{0,1},{1,0},{2,3},{3,2},{4,5},{5,4},{6,7},{7,6},{8,9},{9,8},{10,11... | collective-permute-start | bytes 688136 | tf_op jit(solution)/shard_map/ppermute | solution.py:119
  169.7 9.9 %collective-permute-start.85 = (bf16[32,3584]{1,0:T(8,128)(2,1)S(1)}, bf16[32,3584]{1,0:T(8,128)(2,1)S(1)}, u32[]{:S(2)}, u32[]{:S(2)}) collective-permute-start(bf16[32,3584]{1,0:T(8,128)(2,1)S(1)} %add_convert_fusion.12), channel_id=1, source_target_pairs={{0,8},{16,24},{8,0},{24,16},{1,9},{17,25},{9,1},{25,17},{2,10},{18... | collective-permute-start | bytes 688136 | tf_op jit(solution)/shard_map/ppermute | solution.py:190
  173.9 9.5 %collective-permute-start.92 = (bf16[32,3584]{1,0:T(8,128)(2,1)S(1)}, bf16[32,3584]{1,0:T(8,128)(2,1)S(1)}, u32[]{:S(2)}, u32[]{:S(2)}) collective-permute-start(bf16[32,3584]{1,0:T(8,128)(2,1)S(1)} %add_convert_fusion.9), channel_id=1, source_target_pairs={{0,6},{1,7},{2,4},{3,5},{4,2},{5,3},{6,0},{7,1},{8,14},{9,15},{10,... | collective-permute-start | bytes 688136 | tf_op jit(solution)/shard_map/ppermute | solution.py:119
  175.5 11.6 %collective-permute-start.90 = (bf16[32,3584]{1,0:T(8,128)(2,1)S(1)}, bf16[32,3584]{1,0:T(8,128)(2,1)S(1)}, u32[]{:S(2)}, u32[]{:S(2)}) collective-permute-start(bf16[32,3584]{1,0:T(8,128)(2,1)S(1)} %add_convert_fusion.10), channel_id=1, source_target_pairs={{0,4},{1,5},{2,6},{3,7},{4,0},{5,1},{6,2},{7,3},{8,12},{9,13},{10,... | collective-permute-start | bytes 688136 | tf_op jit(solution)/shard_map/ppermute | solution.py:119
  177.1 11.0 %collective-permute-start.88 = (bf16[32,3584]{1,0:T(8,128)(2,1)S(1)}, bf16[32,3584]{1,0:T(8,128)(2,1)S(1)}, u32[]{:S(2)}, u32[]{:S(2)}) collective-permute-start(bf16[32,3584]{1,0:T(8,128)(2,1)S(1)} %add_convert_fusion.11), channel_id=1, source_target_pairs={{0,2},{1,3},{2,0},{3,1},{4,6},{5,7},{6,4},{7,5},{8,10},{9,11},{10,... | collective-permute-start | bytes 688136 | tf_op jit(solution)/shard_map/ppermute | solution.py:119
  179.6 13.4 %collective-permute-start.94 = (bf16[32,3584]{1,0:T(8,128)(2,1)S(1)}, bf16[32,3584]{1,0:T(8,128)(2,1)S(1)}, u32[]{:S(2)}, u32[]{:S(2)}) collective-permute-start(bf16[32,3584]{1,0:T(8,128)(2,1)S(1)} %collective-permute-done.85.refs_0_), channel_id=1, source_target_pairs={{0,2},{1,3},{2,0},{3,1},{4,6},{5,7},{6,4},{7,5},{8,10},{9,11},{10,... | collective-permute-start | bytes 688136 | tf_op jit(solution)/shard_map/ppermute | solution.py:119
  181.1 12.1 %collective-permute-start.95 = (bf16[32,3584]{1,0:T(8,128)(2,1)S(1)}, bf16[32,3584]{1,0:T(8,128)(2,1)S(1)}, u32[]{:S(2)}, u32[]{:S(2)}) collective-permute-start(bf16[32,3584]{1,0:T(8,128)(2,1)S(1)} %collective-permute-done.85.refs_0_), channel_id=1, source_target_pairs={{0,4},{1,5},{2,6},{3,7},{4,0},{5,1},{6,2},{7,3},{8,12},{9,13},{10,... | collective-permute-start | bytes 688136 | tf_op jit(solution)/shard_map/ppermute | solution.py:119
  183.4 13.5 %collective-permute-start.96 = (bf16[32,3584]{1,0:T(8,128)(2,1)S(1)}, bf16[32,3584]{1,0:T(8,128)(2,1)S(1)}, u32[]{:S(2)}, u32[]{:S(2)}) collective-permute-start(bf16[32,3584]{1,0:T(8,128)(2,1)S(1)} %collective-permute-done.85.refs_0_), channel_id=1, source_target_pairs={{0,6},{1,7},{2,4},{3,5},{4,2},{5,3},{6,0},{7,1},{8,14},{9,15},{10,... | collective-permute-start | bytes 688136 | tf_op jit(solution)/shard_map/ppermute | solution.py:119
  188.3 8.6 %collective-permute-start.93 = (bf16[32,3584]{1,0:T(8,128)(2,1)S(1)}, bf16[32,3584]{1,0:T(8,128)(2,1)S(1)}, u32[]{:S(2)}, u32[]{:S(2)}) collective-permute-start(bf16[32,3584]{1,0:T(8,128)(2,1)S(1)} %add_convert_fusion.8), channel_id=1, source_target_pairs={{0,8},{16,24},{8,0},{24,16},{1,9},{17,25},{9,1},{25,17},{2,10},{18... | collective-permute-start | bytes 688136 | tf_op jit(solution)/shard_map/ppermute | solution.py:190
  188.5 9.9 %collective-permute-start.100 = (bf16[32,3584]{1,0:T(8,128)(2,1)S(1)}, bf16[32,3584]{1,0:T(8,128)(2,1)S(1)}, u32[]{:S(2)}, u32[]{:S(2)}) collective-permute-start(bf16[32,3584]{1,0:T(8,128)(2,1)S(1)} %collective-permute-done.85.refs_0_), channel_id=1, source_target_pairs={{0,1},{1,0},{2,3},{3,2},{4,5},{5,4},{6,7},{7,6},{8,9},{9,8},{10,11... | collective-permute-start | bytes 688136 | tf_op jit(solution)/shard_map/ppermute | solution.py:119
  196.9 12.1 %collective-permute-start.97 = (bf16[32,3584]{1,0:T(8,128)(2,1)S(1)}, bf16[32,3584]{1,0:T(8,128)(2,1)S(1)}, u32[]{:S(2)}, u32[]{:S(2)}) collective-permute-start(bf16[32,3584]{1,0:T(8,128)(2,1)S(1)} %collective-permute-done.93.refs_0_), channel_id=1, source_target_pairs={{0,2},{1,3},{2,0},{3,1},{4,6},{5,7},{6,4},{7,5},{8,10},{9,11},{10,... | collective-permute-start | bytes 688136 | tf_op jit(solution)/shard_map/ppermute | solution.py:119
  198.4 12.7 %collective-permute-start.98 = (bf16[32,3584]{1,0:T(8,128)(2,1)S(1)}, bf16[32,3584]{1,0:T(8,128)(2,1)S(1)}, u32[]{:S(2)}, u32[]{:S(2)}) collective-permute-start(bf16[32,3584]{1,0:T(8,128)(2,1)S(1)} %collective-permute-done.93.refs_0_), channel_id=1, source_target_pairs={{0,4},{1,5},{2,6},{3,7},{4,0},{5,1},{6,2},{7,3},{8,12},{9,13},{10,... | collective-permute-start | bytes 688136 | tf_op jit(solution)/shard_map/ppermute | solution.py:119
  198.9 12.1 %collective-permute-start.99 = (bf16[32,3584]{1,0:T(8,128)(2,1)S(1)}, bf16[32,3584]{1,0:T(8,128)(2,1)S(1)}, u32[]{:S(2)}, u32[]{:S(2)}) collective-permute-start(bf16[32,3584]{1,0:T(8,128)(2,1)S(1)} %collective-permute-done.93.refs_0_), channel_id=1, source_target_pairs={{0,6},{1,7},{2,4},{3,5},{4,2},{5,3},{6,0},{7,1},{8,14},{9,15},{10,... | collective-permute-start | bytes 688136 | tf_op jit(solution)/shard_map/ppermute | solution.py:119
  214.7 12.1 %collective-permute-start.108 = (bf16[32,3584]{1,0:T(8,128)(2,1)S(1)}, bf16[32,3584]{1,0:T(8,128)(2,1)S(1)}, u32[]{:S(2)}, u32[]{:S(2)}) collective-permute-start(bf16[32,3584]{1,0:T(8,128)(2,1)S(1)} %add_convert_fusion.7), channel_id=1, source_target_pairs={{0,2},{1,3},{2,0},{3,1},{4,6},{5,7},{6,4},{7,5},{8,10},{9,11},{10,... | collective-permute-start | bytes 688136 | tf_op jit(solution)/shard_map/ppermute | solution.py:119
  215.2 12.5 %collective-permute-start.109 = (bf16[32,3584]{1,0:T(8,128)(2,1)S(1)}, bf16[32,3584]{1,0:T(8,128)(2,1)S(1)}, u32[]{:S(2)}, u32[]{:S(2)}) collective-permute-start(bf16[32,3584]{1,0:T(8,128)(2,1)S(1)} %add_convert_fusion.6), channel_id=1, source_target_pairs={{0,4},{1,5},{2,6},{3,7},{4,0},{5,1},{6,2},{7,3},{8,12},{9,13},{10,... | collective-permute-start | bytes 688136 | tf_op jit(solution)/shard_map/ppermute | solution.py:119
  216.4 11.3 %collective-permute-start.110 = (bf16[32,3584]{1,0:T(8,128)(2,1)S(1)}, bf16[32,3584]{1,0:T(8,128)(2,1)S(1)}, u32[]{:S(2)}, u32[]{:S(2)}) collective-permute-start(bf16[32,3584]{1,0:T(8,128)(2,1)S(1)} %add_convert_fusion.5), channel_id=1, source_target_pairs={{0,6},{1,7},{2,4},{3,5},{4,2},{5,3},{6,0},{7,1},{8,14},{9,15},{10,... | collective-permute-start | bytes 688136 | tf_op jit(solution)/shard_map/ppermute | solution.py:119
  229.0 7.5 %collective-permute-start.115 = (bf16[32,3584]{1,0:T(8,128)(2,1)S(1)}, bf16[32,3584]{1,0:T(8,128)(2,1)S(1)}, u32[]{:S(2)}, u32[]{:S(2)}) collective-permute-start(bf16[32,3584]{1,0:T(8,128)(2,1)S(1)} %get-tuple-element.371), channel_id=1, source_target_pairs={{0,1},{1,0},{2,3},{3,2},{4,5},{5,4},{6,7},{7,6},{8,9},{9,8},{10,11... | collective-permute-start | bytes 688136 | tf_op jit(solution)/shard_map/ppermute | solution.py:119
  231.4 9.5 %collective-permute-start.121 = (bf16[32,3584]{1,0:T(8,128)(2,1)S(1)}, bf16[32,3584]{1,0:T(8,128)(2,1)S(1)}, u32[]{:S(2)}, u32[]{:S(2)}) collective-permute-start(bf16[32,3584]{1,0:T(8,128)(2,1)S(1)} %add_convert_fusion.1), channel_id=1, source_target_pairs={{0,6},{1,7},{2,4},{3,5},{4,2},{5,3},{6,0},{7,1},{8,14},{9,15},{10,... | collective-permute-start | bytes 688136 | tf_op jit(solution)/shard_map/ppermute | solution.py:119
  232.9 12.0 %collective-permute-start.119 = (bf16[32,3584]{1,0:T(8,128)(2,1)S(1)}, bf16[32,3584]{1,0:T(8,128)(2,1)S(1)}, u32[]{:S(2)}, u32[]{:S(2)}) collective-permute-start(bf16[32,3584]{1,0:T(8,128)(2,1)S(1)} %add_convert_fusion.2), channel_id=1, source_target_pairs={{0,4},{1,5},{2,6},{3,7},{4,0},{5,1},{6,2},{7,3},{8,12},{9,13},{10,... | collective-permute-start | bytes 688136 | tf_op jit(solution)/shard_map/ppermute | solution.py:119
  234.6 10.3 %collective-permute-start.117 = (bf16[32,3584]{1,0:T(8,128)(2,1)S(1)}, bf16[32,3584]{1,0:T(8,128)(2,1)S(1)}, u32[]{:S(2)}, u32[]{:S(2)}) collective-permute-start(bf16[32,3584]{1,0:T(8,128)(2,1)S(1)} %add_convert_fusion.3), channel_id=1, source_target_pairs={{0,2},{1,3},{2,0},{3,1},{4,6},{5,7},{6,4},{7,5},{8,10},{9,11},{10,... | collective-permute-start | bytes 688136 | tf_op jit(solution)/shard_map/ppermute | solution.py:119
  (68 other events, 335.9 us)
where the time goes:
time: 251 us; the launch traced here: 248 us
  starting transfers between devices  83.6 us (33%)
  waiting for transfers between devices  78.5 us (31%)
  Pallas kernels  68.6 us (27%)
  other arithmetic  13.2 us (5%)
    ppermute x116, starting transfers between devices, exchange(): lax.ppermute(block, 'expert', [(i, i ^ mask) for i in range(experts)])  75.7 us
    ppermute x116, waiting for transfers between devices, exchange(): lax.ppermute(block, 'expert', [(i, i ^ mask) for i in range(experts)])  74.5 us
    pallas_call x8, Pallas kernels, expert_call(): pl.pallas_call(functools.partial(expert_kernel, count), out_shape=[jax.Sh...  68.6 us
    ppermute x6, starting transfers between devices, on_device(): entering = [lax.ppermute(block, 'pipe', pairs) for block in leaving]  7.9 us
    convert_element_type x24, other arithmetic, on_chip(): return total[:1] + [part.astype(jnp.bfloat16) for part in total[1:]]  5.72 us
  transfers between devices with their start and end apart: 122, of which 46 were waited for; matrix products, arithmetic and copies ran while one was open for 4% of the time, Pallas kernels for 28%

commit v1 on v0

--- a/solution.py
+++ b/solution.py
@@ -89,7 +89,7 @@
             pltpu.VMEM((hid, width), jnp.bfloat16),
             pltpu.SemaphoreType.DMA((2 * (hid // HIDS) + BLOCKS,)),
         ],
-        compiler_params=pltpu.CompilerParams(vmem_limit_bytes=(24 + count * tokens // 64) * 2**20),
+        compiler_params=pltpu.CompilerParams(vmem_limit_bytes=(20 + count * tokens // 64) * 2**20),
         cost_estimate=pl.CostEstimate(
             flops=6 * slots * width * hid, bytes_accessed=6 * width * hid, transcendentals=slots * hid
         ),
@@ -119,10 +119,12 @@
         return lax.ppermute(block, "expert", [(i, i ^ mask) for i in range(experts)])
 
     def on_chip(outs):
+        mine, other = outs[1:half] + outs[:1], outs[half + 1 :] + outs[half : half + 1]
         total = [
             a.astype(jnp.float32) + exchange(b, 1).astype(jnp.float32)
-            for a, b in zip(outs[:half], outs[half:])
+            for a, b in zip(mine, other)
         ]
+        total = total[-1:] + total[:-1]
         return total[:1] + [part.astype(jnp.bfloat16) for part in total[1:]]
 
     def send_back(sums):
@@ -157,7 +159,7 @@
     results = []
     for tick in range(planes):
         stream = 0 if tick < planes // 2 else 1
-        near, sums, back = [], [], []
+        near, sums, back, leaving = [], [], [], []
         for m in range(micros):
             own = entering[m]
             if m > 0:
@@ -175,14 +177,17 @@
             )
             if m > 0:
                 back[m - 1], outs = after(back[m - 1], outs)
+                total = entering[m - 1].astype(jnp.float32)
+                for part in back[m - 1]:
+                    total += part.astype(jnp.float32)
+                done, outs = after(total.astype(jnp.bfloat16), outs)
+                leaving.append(done)
         sums.append(on_chip(outs))
         back.append(send_back(sums[-1]))
-        leaving = []
-        for m in range(micros):
-            total = entering[m].astype(jnp.float32)
-            for part in back[m]:
-                total += part.astype(jnp.float32)
-            leaving.append(total.astype(jnp.bfloat16))
+        total = entering[-1].astype(jnp.float32)
+        for part in back[-1]:
+            total += part.astype(jnp.float32)
+        leaving.append(total.astype(jnp.bfloat16))
         results.append(leaving)
         if tick + 1 < planes:
             ups = [(p, p + 1) for p in range(tick % 2, planes - 1, 2)]

time: 251 us -> 249 us (level)
  transfers between devices with their start and end apart: 122 -> 122, of which waited for: 46 -> 47; matrix products, arithmetic and copies ran while one was open for 4% -> 4% of each run, Pallas kernels for 28% -> 28%
where the time goes in v1:
time: 249 us; the launch traced here: 246 us
  starting transfers between devices  83.7 us (34%)
  waiting for transfers between devices  78.1 us (31%)
  Pallas kernels  68.6 us (28%)
  other arithmetic  11.1 us (4%)
  local copies, waits for them, and re-layouts  2.72 us (1%)
    ppermute x116, starting transfers between devices, exchange(): lax.ppermute(block, 'expert', [(i, i ^ mask) for i in range(experts)])  75.7 us
    ppermute x116, waiting for transfers between devices, exchange(): lax.ppermute(block, 'expert', [(i, i ^ mask) for i in range(experts)])  74 us
    pallas_call x8, Pallas kernels, expert_call(): pl.pallas_call(functools.partial(expert_kernel, count), out_shape=[jax.Sh...  68.6 us
    ppermute x6, starting transfers between devices, on_device(): entering = [lax.ppermute(block, 'pipe', pairs) for block in leaving]  7.97 us
    convert_element_type x24, other arithmetic, on_chip(): return total[:1] + [part.astype(jnp.bfloat16) for part in total[1:]]  6.15 us
  transfers between devices with their start and end apart: 122, of which 47 were waited for; matrix products, arithmetic and copies ran while one was open for 4% of the time, Pallas kernels for 28%

profile of v1, /device:TPU:0, one launch (start us, length us, event | category | flops | bytes accessed | tf_op | source)
XLA Modules:
  0.0 245.9 jit_solution(1535628641990611067)
XLA Ops:
  1.9 1.3 select_bitcast_fusion.1
  3.3 2.6 %collective-permute-start = (bf16[32,3584]{1,0:T(8,128)(2,1)S(1)}, bf16[32,3584]{1,0:T(8,128)(2,1)S(1)}, u32[]{:S(2)}, u32[]{:S(2)}) collective-permute-start(bf16[32,3584]{1,0:T(8,128)(2,1)S(1)} %get-tuple-element.454.refs_0_), channel_id=1, source_target_pairs={{0,2},{1,3},{2,0},{3,1},{4,6},{5,7},{6,4},{7,5},{8,10},{9,11},{10,... | collective-permute-start | bytes 688136 | tf_op jit(solution)/shard_map/ppermute | solution.py:119
  5.8 1.5 collective-permute-start.1
  7.5 2.0 collective-permute-start.12
  9.4 1.5 collective-permute-start.11
  10.9 3.0 %collective-permute-done.13 = f32[2,2,2,2,32,2]{4,5,3,2,1,0:T(2,128)S(1)} collective-permute-done((f32[2,2,2,2,32,2]{4,5,3,2,1,0:T(2,128)S(1)}, f32[2,2,2,2,32,2]{4,5,3,2,1,0:T(2,128)S(1)}, u32[]{:S(2)}, u32[]{:S(2)}) %collective-permute-start.13) | collective-permute-done | bytes 4128 | tf_op jit(solution)/shard_map/ppermute | solution.py:119
  13.9 1.4 collective-permute-start.2
  17.5 4.0 %collective-permute-done.2.refs_3_ = bf16[32,3584]{1,0:T(8,128)(2,1)S(1)} collective-permute-done((bf16[32,3584]{1,0:T(8,128)(2,1)S(1)}, bf16[32,3584]{1,0:T(8,128)(2,1)S(1)}, u32[]{:S(2)}, u32[]{:S(2)}) %collective-permute-start.2) | collective-permute-done | bytes 229408 | tf_op jit(solution)/shard_map/ppermute | solution.py:119
  21.5 1.6 collective-permute-start.3
  23.6 1.5 collective-permute-start.5
  25.8 8.6 %shard_map.113 = (bf16[32,3584]{1,0:T(8,128)(2,1)S(1)}, bf16[32,3584]{1,0:T(8,128)(2,1)S(1)}, bf16[32,3584]{1,0:T(8,128)(2,1)S(1)}, bf16[32,3584]{1,0:T(8,128)(2...) custom-call(bf16[32,3584]{1,0:T(8,128)(2,1)S(1)} %get-tuple-element., ...), custom_call_target="tpu_custom_call" | custom-call | flops 2818572288 | bytes 22020096 | tf_op jit(solution)/shard_map/pallas_call | solution.py:78
  34.4 1.3 collective-permute-done.4.refs_2_
  42.9 1.8 collective-permute-start.20
  44.7 8.6 %shard_map.114 = (bf16[32,3584]{1,0:T(8,128)(2,1)S(1)}, bf16[32,3584]{1,0:T(8,128)(2,1)S(1)}, bf16[32,3584]{1,0:T(8,128)(2,1)S(1)}, bf16[32,3584]{1,0:T(8,128)(2...) custom-call(bf16[32,3584]{1,0:T(8,128)(2,1)S(1)} %get-tuple-element., ...), custom_call_target="tpu_custom_call" | custom-call | flops 2818572288 | bytes 22020096 | tf_op jit(solution)/shard_map/pallas_call | solution.py:78
  55.6 1.6 collective-permute-start.25
  57.3 1.5 collective-permute-start.32
  58.8 1.6 collective-permute-start.30
  61.1 2.1 collective-permute-done.25.refs_0_
  63.2 1.5 collective-permute-start.34
  65.2 1.6 collective-permute-done.32
  66.8 1.4 collective-permute-start.36
  68.2 2.3 collective-permute-done.30
  72.1 4.2 %collective-permute-done.34.refs_1_ = bf16[32,3584]{1,0:T(8,128)(2,1)S(1)} collective-permute-done((bf16[32,3584]{1,0:T(8,128)(2,1)S(1)}, bf16[32,3584]{1,0:T(8,128)(2,1)S(1)}, u32[]{:S(2)}, u32[]{:S(2)}) %collective-permute-start.34) | collective-permute-done | bytes 229408 | tf_op jit(solution)/shard_map/ppermute | solution.py:119
  76.9 3.5 %collective-permute-done.36.refs_3_ = bf16[32,3584]{1,0:T(8,128)(2,1)S(1)} collective-permute-done((bf16[32,3584]{1,0:T(8,128)(2,1)S(1)}, bf16[32,3584]{1,0:T(8,128)(2,1)S(1)}, u32[]{:S(2)}, u32[]{:S(2)}) %collective-permute-start.36) | collective-permute-done | bytes 229408 | tf_op jit(solution)/shard_map/ppermute | solution.py:119
  80.3 1.5 collective-permute-start.37
  82.3 1.5 collective-permute-start.39
  83.8 8.6 %shard_map.115 = (bf16[32,3584]{1,0:T(8,128)(2,1)S(1)}, bf16[32,3584]{1,0:T(8,128)(2,1)S(1)}, bf16[32,3584]{1,0:T(8,128)(2,1)S(1)}, bf16[32,3584]{1,0:T(8,128)(2...) custom-call(bf16[32,3584]{1,0:T(8,128)(2,1)S(1)} %collective-permute, ...), custom_call_target="tpu_custom_call" | custom-call | flops 2818572288 | bytes 22020096 | tf_op jit(solution)/shard_map/pallas_call | solution.py:78
  92.4 2.0 collective-permute-done.38.refs_2_
  99.9 1.8 collective-permute-start.50
  101.6 8.6 %shard_map.116 = (bf16[32,3584]{1,0:T(8,128)(2,1)S(1)}, bf16[32,3584]{1,0:T(8,128)(2,1)S(1)}, bf16[32,3584]{1,0:T(8,128)(2,1)S(1)}, bf16[32,3584]{1,0:T(8,128)(2...) custom-call(bf16[32,3584]{1,0:T(8,128)(2,1)S(1)} %collective-permute, ...), custom_call_target="tpu_custom_call" | custom-call | flops 2818572288 | bytes 22020096 | tf_op jit(solution)/shard_map/pallas_call | solution.py:78
  113.1 1.5 collective-permute-start.61
  114.7 1.6 collective-permute-start.59
  116.9 1.5 collective-permute-start.64
  118.9 3.6 %collective-permute-done.61 = bf16[32,3584]{1,0:T(8,128)(2,1)S(1)} collective-permute-done((bf16[32,3584]{1,0:T(8,128)(2,1)S(1)}, bf16[32,3584]{1,0:T(8,128)(2,1)S(1)}, u32[]{:S(2)}, u32[]{:S(2)}) %collective-permute-start.61) | collective-permute-done | bytes 229408 | tf_op jit(solution)/shard_map/ppermute | solution.py:119
  122.6 1.4 collective-permute-start.66
  124.0 2.7 %collective-permute-done.59 = bf16[32,3584]{1,0:T(8,128)(2,1)S(1)} collective-permute-done((bf16[32,3584]{1,0:T(8,128)(2,1)S(1)}, bf16[32,3584]{1,0:T(8,128)(2,1)S(1)}, u32[]{:S(2)}, u32[]{:S(2)}) %collective-permute-start.59) | collective-permute-done | bytes 229408 | tf_op jit(solution)/shard_map/ppermute | solution.py:119
  128.2 4.0 %collective-permute-done.64.refs_1_ = bf16[32,3584]{1,0:T(8,128)(2,1)S(1)} collective-permute-done((bf16[32,3584]{1,0:T(8,128)(2,1)S(1)}, bf16[32,3584]{1,0:T(8,128)(2,1)S(1)}, u32[]{:S(2)}, u32[]{:S(2)}) %collective-permute-start.64) | collective-permute-done | bytes 229408 | tf_op jit(solution)/shard_map/ppermute | solution.py:119
  132.7 3.8 %collective-permute-done.66.refs_3_ = bf16[32,3584]{1,0:T(8,128)(2,1)S(1)} collective-permute-done((bf16[32,3584]{1,0:T(8,128)(2,1)S(1)}, bf16[32,3584]{1,0:T(8,128)(2,1)S(1)}, u32[]{:S(2)}, u32[]{:S(2)}) %collective-permute-start.66) | collective-permute-done | bytes 229408 | tf_op jit(solution)/shard_map/ppermute | solution.py:119
  136.6 1.6 collective-permute-start.67
  138.7 1.5 collective-permute-start.69
  140.2 8.6 %shard_map.117 = (bf16[32,3584]{1,0:T(8,128)(2,1)S(1)}, bf16[32,3584]{1,0:T(8,128)(2,1)S(1)}, bf16[32,3584]{1,0:T(8,128)(2,1)S(1)}, bf16[32,3584]{1,0:T(8,128)(2...) custom-call(bf16[32,3584]{1,0:T(8,128)(2,1)S(1)} %collective-permute, ...), custom_call_target="tpu_custom_call" | custom-call | flops 2818572288 | bytes 22020096 | tf_op jit(solution)/shard_map/pallas_call | solution.py:78
  148.8 2.0 collective-permute-done.68.refs_2_
  157.4 1.8 collective-permute-start.80
  159.2 8.6 %shard_map.118 = (bf16[32,3584]{1,0:T(8,128)(2,1)S(1)}, bf16[32,3584]{1,0:T(8,128)(2,1)S(1)}, bf16[32,3584]{1,0:T(8,128)(2,1)S(1)}, bf16[32,3584]{1,0:T(8,128)(2...) custom-call(bf16[32,3584]{1,0:T(8,128)(2,1)S(1)} %collective-permute, ...), custom_call_target="tpu_custom_call" | custom-call | flops 2818572288 | bytes 22020096 | tf_op jit(solution)/shard_map/pallas_call | solution.py:78
  170.1 4.1 %collective-permute-start.85 = (bf16[32,3584]{1,0:T(8,128)(2,1)S(1)}, bf16[32,3584]{1,0:T(8,128)(2,1)S(1)}, u32[]{:S(2)}, u32[]{:S(2)}) collective-permute-start(bf16[32,3584]{1,0:T(8,128)(2,1)S(1)} %add_convert_fusion.12), channel_id=1, source_target_pairs={{0,8},{16,24},{8,0},{24,16},{1,9},{17,25},{9,1},{25,17},{2,10},{18... | collective-permute-start | bytes 688136 | tf_op jit(solution)/shard_map/ppermute | solution.py:195
  174.3 1.5 collective-permute-start.92
  175.9 1.6 collective-permute-start.90
  178.1 2.0 collective-permute-done.85.refs_0_
  180.1 1.5 collective-permute-start.94
  182.1 1.7 collective-permute-done.92
  183.8 1.4 collective-permute-start.96
  185.3 2.3 collective-permute-done.90
  189.1 4.3 %collective-permute-done.94.refs_1_ = bf16[32,3584]{1,0:T(8,128)(2,1)S(1)} collective-permute-done((bf16[32,3584]{1,0:T(8,128)(2,1)S(1)}, bf16[32,3584]{1,0:T(8,128)(2,1)S(1)}, u32[]{:S(2)}, u32[]{:S(2)}) %collective-permute-start.94) | collective-permute-done | bytes 229408 | tf_op jit(solution)/shard_map/ppermute | solution.py:119
  193.9 3.5 %collective-permute-done.96.refs_3_ = bf16[32,3584]{1,0:T(8,128)(2,1)S(1)} collective-permute-done((bf16[32,3584]{1,0:T(8,128)(2,1)S(1)}, bf16[32,3584]{1,0:T(8,128)(2,1)S(1)}, u32[]{:S(2)}, u32[]{:S(2)}) %collective-permute-start.96) | collective-permute-done | bytes 229408 | tf_op jit(solution)/shard_map/ppermute | solution.py:119
  197.4 1.5 collective-permute-start.97
  199.4 1.5 collective-permute-start.99
  200.9 8.6 %shard_map.119 = (bf16[32,3584]{1,0:T(8,128)(2,1)S(1)}, bf16[32,3584]{1,0:T(8,128)(2,1)S(1)}, bf16[32,3584]{1,0:T(8,128)(2,1)S(1)}, bf16[32,3584]{1,0:T(8,128)(2...) custom-call(bf16[32,3584]{1,0:T(8,128)(2,1)S(1)} %collective-permute, ...), custom_call_target="tpu_custom_call" | custom-call | flops 2818572288 | bytes 22020096 | tf_op jit(solution)/shard_map/pallas_call | solution.py:78
  209.5 2.0 collective-permute-done.98.refs_2_
  216.9 1.8 collective-permute-start.110
  218.7 8.6 %shard_map.120 = (bf16[32,3584]{1,0:T(8,128)(2,1)S(1)}, bf16[32,3584]{1,0:T(8,128)(2,1)S(1)}, bf16[32,3584]{1,0:T(8,128)(2,1)S(1)}, bf16[32,3584]{1,0:T(8,128)(2...) custom-call(bf16[32,3584]{1,0:T(8,128)(2,1)S(1)} %collective-permute, ...), custom_call_target="tpu_custom_call" | custom-call | flops 2818572288 | bytes 22020096 | tf_op jit(solution)/shard_map/pallas_call | solution.py:78
  230.6 1.4 collective-permute-start.121
  232.8 1.5 collective-permute-start.119
  235.6 4.6 %collective-permute-done.121 = bf16[32,3584]{1,0:T(8,128)(2,1)S(1)} collective-permute-done((bf16[32,3584]{1,0:T(8,128)(2,1)}, bf16[32,3584]{1,0:T(8,128)(2,1)S(1)}, u32[]{:S(2)}, u32[]{:S(2)}) %collective-permute-start.121) | collective-permute-done | bytes 229408 | tf_op jit(solution)/shard_map/ppermute | solution.py:119
  240.2 4.1 %collective-permute-done.119 = bf16[32,3584]{1,0:T(8,128)(2,1)S(1)} collective-permute-done((bf16[32,3584]{1,0:T(8,128)(2,1)}, bf16[32,3584]{1,0:T(8,128)(2,1)S(1)}, u32[]{:S(2)}, u32[]{:S(2)}) %collective-permute-start.119) | collective-permute-done | bytes 229408 | tf_op jit(solution)/shard_map/ppermute | solution.py:119
  (267 shorter events, 55.0 us)
Async XLA Ops:
  3.3 13.6 %collective-permute-start = (bf16[32,3584]{1,0:T(8,128)(2,1)S(1)}, bf16[32,3584]{1,0:T(8,128)(2,1)S(1)}, u32[]{:S(2)}, u32[]{:S(2)}) collective-permute-start(bf16[32,3584]{1,0:T(8,128)(2,1)S(1)} %get-tuple-element.454.refs_0_), channel_id=1, source_target_pairs={{0,2},{1,3},{2,0},{3,1},{4,6},{5,7},{6,4},{7,5},{8,10},{9,11},{10,... | collective-permute-start | bytes 688136 | tf_op jit(solution)/shard_map/ppermute | solution.py:119
  5.8 11.6 %collective-permute-start.1 = (bf16[32,3584]{1,0:T(8,128)(2,1)S(1)}, bf16[32,3584]{1,0:T(8,128)(2,1)S(1)}, u32[]{:S(2)}, u32[]{:S(2)}) collective-permute-start(bf16[32,3584]{1,0:T(8,128)(2,1)S(1)} %get-tuple-element.454.refs_0_), channel_id=1, source_target_pairs={{0,4},{1,5},{2,6},{3,7},{4,0},{5,1},{6,2},{7,3},{8,12},{9,13},{10,... | collective-permute-start | bytes 688136 | tf_op jit(solution)/shard_map/ppermute | solution.py:119
  7.5 7.9 %collective-permute-start.12 = (f32[2,2,2,2,32,2]{4,5,3,2,1,0:T(2,128)S(1)}, f32[2,2,2,2,32,2]{4,5,3,2,1,0:T(2,128)S(1)}, u32[]{:S(2)}, u32[]{:S(2)}) collective-permute-start(f32[2,2,2,2,32,2]{4,5,3,2,1,0:T(2,128)S(1)} %get-tuple-element.465), channel_id=1, source_target_pairs={{0,4},{1,5},{2,6},{3,7},{4,0},{5,1},{6,2},{7,3},{8,12},{9,13},{10,... | collective-permute-start | bytes 12296 | tf_op jit(solution)/shard_map/ppermute | solution.py:119
  13.9 7.5 %collective-permute-start.2 = (bf16[32,3584]{1,0:T(8,128)(2,1)S(1)}, bf16[32,3584]{1,0:T(8,128)(2,1)S(1)}, u32[]{:S(2)}, u32[]{:S(2)}) collective-permute-start(bf16[32,3584]{1,0:T(8,128)(2,1)S(1)} %get-tuple-element.454.refs_0_), channel_id=1, source_target_pairs={{0,6},{1,7},{2,4},{3,5},{4,2},{5,3},{6,0},{7,1},{8,14},{9,15},{10,... | collective-permute-start | bytes 688136 | tf_op jit(solution)/shard_map/ppermute | solution.py:119
  15.4 7.7 %collective-permute-start.6 = (bf16[32,3584]{1,0:T(8,128)(2,1)S(1)}, bf16[32,3584]{1,0:T(8,128)(2,1)S(1)}, u32[]{:S(2)}, u32[]{:S(2)}) collective-permute-start(bf16[32,3584]{1,0:T(8,128)(2,1)S(1)} %get-tuple-element.454.refs_0_), channel_id=1, source_target_pairs={{0,1},{1,0},{2,3},{3,2},{4,5},{5,4},{6,7},{7,6},{8,9},{9,8},{10,11... | collective-permute-start | bytes 688136 | tf_op jit(solution)/shard_map/ppermute | solution.py:119
  17.4 7.6 %collective-permute-start.8 = (bf16[32,3584]{1,0:T(8,128)(2,1)S(1)}, bf16[32,3584]{1,0:T(8,128)(2,1)S(1)}, u32[]{:S(2)}, u32[]{:S(2)}) collective-permute-start(bf16[32,3584]{1,0:T(8,128)(2,1)S(1)} %collective-permute-done.1.refs_2_), channel_id=1, source_target_pairs={{0,1},{1,0},{2,3},{3,2},{4,5},{5,4},{6,7},{7,6},{8,9},{9,8},{10,11... | collective-permute-start | bytes 688136 | tf_op jit(solution)/shard_map/ppermute | solution.py:119
  21.5 12.9 %collective-permute-start.3 = (bf16[32,3584]{1,0:T(8,128)(2,1)S(1)}, bf16[32,3584]{1,0:T(8,128)(2,1)S(1)}, u32[]{:S(2)}, u32[]{:S(2)}) collective-permute-start(bf16[32,3584]{1,0:T(8,128)(2,1)S(1)} %get-tuple-element.226.refs_0_), channel_id=1, source_target_pairs={{0,2},{1,3},{2,0},{3,1},{4,6},{5,7},{6,4},{7,5},{8,10},{9,11},{10,... | collective-permute-start | bytes 688136 | tf_op jit(solution)/shard_map/ppermute | solution.py:119
  23.1 12.7 %collective-permute-start.4 = (bf16[32,3584]{1,0:T(8,128)(2,1)S(1)}, bf16[32,3584]{1,0:T(8,128)(2,1)S(1)}, u32[]{:S(2)}, u32[]{:S(2)}) collective-permute-start(bf16[32,3584]{1,0:T(8,128)(2,1)S(1)} %get-tuple-element.226.refs_0_), channel_id=1, source_target_pairs={{0,4},{1,5},{2,6},{3,7},{4,0},{5,1},{6,2},{7,3},{8,12},{9,13},{10,... | collective-permute-start | bytes 688136 | tf_op jit(solution)/shard_map/ppermute | solution.py:119
  23.6 12.1 %collective-permute-start.5 = (bf16[32,3584]{1,0:T(8,128)(2,1)S(1)}, bf16[32,3584]{1,0:T(8,128)(2,1)S(1)}, u32[]{:S(2)}, u32[]{:S(2)}) collective-permute-start(bf16[32,3584]{1,0:T(8,128)(2,1)S(1)} %get-tuple-element.226.refs_0_), channel_id=1, source_target_pairs={{0,6},{1,7},{2,4},{3,5},{4,2},{5,3},{6,0},{7,1},{8,14},{9,15},{10,... | collective-permute-start | bytes 688136 | tf_op jit(solution)/shard_map/ppermute | solution.py:119
  41.1 12.2 %collective-permute-start.18 = (bf16[32,3584]{1,0:T(8,128)(2,1)S(1)}, bf16[32,3584]{1,0:T(8,128)(2,1)S(1)}, u32[]{:S(2)}, u32[]{:S(2)}) collective-permute-start(bf16[32,3584]{1,0:T(8,128)(2,1)S(1)} %add_convert_fusion.31), channel_id=1, source_target_pairs={{0,2},{1,3},{2,0},{3,1},{4,6},{5,7},{6,4},{7,5},{8,10},{9,11},{10,... | collective-permute-start | bytes 688136 | tf_op jit(solution)/shard_map/ppermute | solution.py:119
  41.7 12.7 %collective-permute-start.19 = (bf16[32,3584]{1,0:T(8,128)(2,1)}, bf16[32,3584]{1,0:T(8,128)(2,1)S(1)}, u32[]{:S(2)}, u32[]{:S(2)}) collective-permute-start(bf16[32,3584]{1,0:T(8,128)(2,1)} %add_convert_fusion.30), channel_id=1, source_target_pairs={{0,4},{1,5},{2,6},{3,7},{4,0},{5,1},{6,2},{7,3},{8,12},{9,13},{10,... | collective-permute-start | bytes 688136 | tf_op jit(solution)/shard_map/ppermute | solution.py:119
  42.9 11.5 %collective-permute-start.20 = (bf16[32,3584]{1,0:T(8,128)(2,1)}, bf16[32,3584]{1,0:T(8,128)(2,1)S(1)}, u32[]{:S(2)}, u32[]{:S(2)}) collective-permute-start(bf16[32,3584]{1,0:T(8,128)(2,1)} %add_convert_fusion.29), channel_id=1, source_target_pairs={{0,6},{1,7},{2,4},{3,5},{4,2},{5,3},{6,0},{7,1},{8,14},{9,15},{10,... | collective-permute-start | bytes 688136 | tf_op jit(solution)/shard_map/ppermute | solution.py:119
  55.2 9.5 %collective-permute-start.26 = (bf16[32,3584]{1,0:T(8,128)(2,1)S(1)}, bf16[32,3584]{1,0:T(8,128)(2,1)S(1)}, u32[]{:S(2)}, u32[]{:S(2)}) collective-permute-start(bf16[32,3584]{1,0:T(8,128)(2,1)S(1)} %get-tuple-element.275), channel_id=1, source_target_pairs={{0,1},{1,0},{2,3},{3,2},{4,5},{5,4},{6,7},{7,6},{8,9},{9,8},{10,11... | collective-permute-start | bytes 688136 | tf_op jit(solution)/shard_map/ppermute | solution.py:119
  55.6 7.6 %collective-permute-start.25 = (bf16[32,3584]{1,0:T(8,128)(2,1)S(1)}, bf16[32,3584]{1,0:T(8,128)(2,1)S(1)}, u32[]{:S(2)}, u32[]{:S(2)}) collective-permute-start(bf16[32,3584]{1,0:T(8,128)(2,1)S(1)} %add_convert_fusion.28), channel_id=1, source_target_pairs={{0,8},{16,24},{8,0},{24,16},{1,9},{17,25},{9,1},{25,17},{2,10},{18... | collective-permute-start | bytes 688136 | tf_op jit(solution)/shard_map/ppermute | solution.py:195
  57.3 9.5 %collective-permute-start.32 = (bf16[32,3584]{1,0:T(8,128)(2,1)S(1)}, bf16[32,3584]{1,0:T(8,128)(2,1)S(1)}, u32[]{:S(2)}, u32[]{:S(2)}) collective-permute-start(bf16[32,3584]{1,0:T(8,128)(2,1)S(1)} %add_convert_fusion.25), channel_id=1, source_target_pairs={{0,6},{1,7},{2,4},{3,5},{4,2},{5,3},{6,0},{7,1},{8,14},{9,15},{10,... | collective-permute-start | bytes 688136 | tf_op jit(solution)/shard_map/ppermute | solution.py:119
  58.8 11.7 %collective-permute-start.30 = (bf16[32,3584]{1,0:T(8,128)(2,1)S(1)}, bf16[32,3584]{1,0:T(8,128)(2,1)S(1)}, u32[]{:S(2)}, u32[]{:S(2)}) collective-permute-start(bf16[32,3584]{1,0:T(8,128)(2,1)S(1)} %add_convert_fusion.26), channel_id=1, source_target_pairs={{0,4},{1,5},{2,6},{3,7},{4,0},{5,1},{6,2},{7,3},{8,12},{9,13},{10,... | collective-permute-start | bytes 688136 | tf_op jit(solution)/shard_map/ppermute | solution.py:119
  60.5 10.9 %collective-permute-start.28 = (bf16[32,3584]{1,0:T(8,128)(2,1)S(1)}, bf16[32,3584]{1,0:T(8,128)(2,1)S(1)}, u32[]{:S(2)}, u32[]{:S(2)}) collective-permute-start(bf16[32,3584]{1,0:T(8,128)(2,1)S(1)} %add_convert_fusion.27), channel_id=1, source_target_pairs={{0,2},{1,3},{2,0},{3,1},{4,6},{5,7},{6,4},{7,5},{8,10},{9,11},{10,... | collective-permute-start | bytes 688136 | tf_op jit(solution)/shard_map/ppermute | solution.py:119
  63.2 13.1 %collective-permute-start.34 = (bf16[32,3584]{1,0:T(8,128)(2,1)S(1)}, bf16[32,3584]{1,0:T(8,128)(2,1)S(1)}, u32[]{:S(2)}, u32[]{:S(2)}) collective-permute-start(bf16[32,3584]{1,0:T(8,128)(2,1)S(1)} %collective-permute-done.25.refs_0_), channel_id=1, source_target_pairs={{0,2},{1,3},{2,0},{3,1},{4,6},{5,7},{6,4},{7,5},{8,10},{9,11},{10,... | collective-permute-start | bytes 688136 | tf_op jit(solution)/shard_map/ppermute | solution.py:119
  64.7 11.8 %collective-permute-start.35 = (bf16[32,3584]{1,0:T(8,128)(2,1)S(1)}, bf16[32,3584]{1,0:T(8,128)(2,1)S(1)}, u32[]{:S(2)}, u32[]{:S(2)}) collective-permute-start(bf16[32,3584]{1,0:T(8,128)(2,1)S(1)} %collective-permute-done.25.refs_0_), channel_id=1, source_target_pairs={{0,4},{1,5},{2,6},{3,7},{4,0},{5,1},{6,2},{7,3},{8,12},{9,13},{10,... | collective-permute-start | bytes 688136 | tf_op jit(solution)/shard_map/ppermute | solution.py:119
  66.8 13.6 %collective-permute-start.36 = (bf16[32,3584]{1,0:T(8,128)(2,1)S(1)}, bf16[32,3584]{1,0:T(8,128)(2,1)S(1)}, u32[]{:S(2)}, u32[]{:S(2)}) collective-permute-start(bf16[32,3584]{1,0:T(8,128)(2,1)S(1)} %collective-permute-done.25.refs_0_), channel_id=1, source_target_pairs={{0,6},{1,7},{2,4},{3,5},{4,2},{5,3},{6,0},{7,1},{8,14},{9,15},{10,... | collective-permute-start | bytes 688136 | tf_op jit(solution)/shard_map/ppermute | solution.py:119
  71.6 8.7 %collective-permute-start.33 = (bf16[32,3584]{1,0:T(8,128)(2,1)S(1)}, bf16[32,3584]{1,0:T(8,128)(2,1)S(1)}, u32[]{:S(2)}, u32[]{:S(2)}) collective-permute-start(bf16[32,3584]{1,0:T(8,128)(2,1)S(1)} %add_convert_fusion.24), channel_id=1, source_target_pairs={{0,8},{16,24},{8,0},{24,16},{1,9},{17,25},{9,1},{25,17},{2,10},{18... | collective-permute-start | bytes 688136 | tf_op jit(solution)/shard_map/ppermute | solution.py:195
  72.1 9.7 %collective-permute-start.40 = (bf16[32,3584]{1,0:T(8,128)(2,1)S(1)}, bf16[32,3584]{1,0:T(8,128)(2,1)S(1)}, u32[]{:S(2)}, u32[]{:S(2)}) collective-permute-start(bf16[32,3584]{1,0:T(8,128)(2,1)S(1)} %collective-permute-done.25.refs_0_), channel_id=1, source_target_pairs={{0,1},{1,0},{2,3},{3,2},{4,5},{5,4},{6,7},{7,6},{8,9},{9,8},{10,11... | collective-permute-start | bytes 688136 | tf_op jit(solution)/shard_map/ppermute | solution.py:119
  76.5 7.3 %collective-permute-start.42 = (bf16[32,3584]{1,0:T(8,128)(2,1)S(1)}, bf16[32,3584]{1,0:T(8,128)(2,1)S(1)}, u32[]{:S(2)}, u32[]{:S(2)}) collective-permute-start(bf16[32,3584]{1,0:T(8,128)(2,1)S(1)} %collective-permute-done.35.refs_2_), channel_id=1, source_target_pairs={{0,1},{1,0},{2,3},{3,2},{4,5},{5,4},{6,7},{7,6},{8,9},{9,8},{10,11... | collective-permute-start | bytes 688136 | tf_op jit(solution)/shard_map/ppermute | solution.py:119
  80.3 12.1 %collective-permute-start.37 = (bf16[32,3584]{1,0:T(8,128)(2,1)S(1)}, bf16[32,3584]{1,0:T(8,128)(2,1)S(1)}, u32[]{:S(2)}, u32[]{:S(2)}) collective-permute-start(bf16[32,3584]{1,0:T(8,128)(2,1)S(1)} %collective-permute-done.33.refs_0_), channel_id=1, source_target_pairs={{0,2},{1,3},{2,0},{3,1},{4,6},{5,7},{6,4},{7,5},{8,10},{9,11},{10,... | collective-permute-start | bytes 688136 | tf_op jit(solution)/shard_map/ppermute | solution.py:119
  81.8 12.7 %collective-permute-start.38 = (bf16[32,3584]{1,0:T(8,128)(2,1)S(1)}, bf16[32,3584]{1,0:T(8,128)(2,1)S(1)}, u32[]{:S(2)}, u32[]{:S(2)}) collective-permute-start(bf16[32,3584]{1,0:T(8,128)(2,1)S(1)} %collective-permute-done.33.refs_0_), channel_id=1, source_target_pairs={{0,4},{1,5},{2,6},{3,7},{4,0},{5,1},{6,2},{7,3},{8,12},{9,13},{10,... | collective-permute-start | bytes 688136 | tf_op jit(solution)/shard_map/ppermute | solution.py:119
  82.3 12.1 %collective-permute-start.39 = (bf16[32,3584]{1,0:T(8,128)(2,1)S(1)}, bf16[32,3584]{1,0:T(8,128)(2,1)S(1)}, u32[]{:S(2)}, u32[]{:S(2)}) collective-permute-start(bf16[32,3584]{1,0:T(8,128)(2,1)S(1)} %collective-permute-done.33.refs_0_), channel_id=1, source_target_pairs={{0,6},{1,7},{2,4},{3,5},{4,2},{5,3},{6,0},{7,1},{8,14},{9,15},{10,... | collective-permute-start | bytes 688136 | tf_op jit(solution)/shard_map/ppermute | solution.py:119
  98.1 12.1 %collective-permute-start.48 = (bf16[32,3584]{1,0:T(8,128)(2,1)S(1)}, bf16[32,3584]{1,0:T(8,128)(2,1)S(1)}, u32[]{:S(2)}, u32[]{:S(2)}) collective-permute-start(bf16[32,3584]{1,0:T(8,128)(2,1)S(1)} %add_convert_fusion.23), channel_id=1, source_target_pairs={{0,2},{1,3},{2,0},{3,1},{4,6},{5,7},{6,4},{7,5},{8,10},{9,11},{10,... | collective-permute-start | bytes 688136 | tf_op jit(solution)/shard_map/ppermute | solution.py:119
  98.7 12.5 %collective-permute-start.49 = (bf16[32,3584]{1,0:T(8,128)(2,1)S(1)}, bf16[32,3584]{1,0:T(8,128)(2,1)S(1)}, u32[]{:S(2)}, u32[]{:S(2)}) collective-permute-start(bf16[32,3584]{1,0:T(8,128)(2,1)S(1)} %add_convert_fusion.22), channel_id=1, source_target_pairs={{0,4},{1,5},{2,6},{3,7},{4,0},{5,1},{6,2},{7,3},{8,12},{9,13},{10,... | collective-permute-start | bytes 688136 | tf_op jit(solution)/shard_map/ppermute | solution.py:119
  99.9 11.3 %collective-permute-start.50 = (bf16[32,3584]{1,0:T(8,128)(2,1)S(1)}, bf16[32,3584]{1,0:T(8,128)(2,1)S(1)}, u32[]{:S(2)}, u32[]{:S(2)}) collective-permute-start(bf16[32,3584]{1,0:T(8,128)(2,1)S(1)} %add_convert_fusion.21), channel_id=1, source_target_pairs={{0,6},{1,7},{2,4},{3,5},{4,2},{5,3},{6,0},{7,1},{8,14},{9,15},{10,... | collective-permute-start | bytes 688136 | tf_op jit(solution)/shard_map/ppermute | solution.py:119
  113.1 9.5 %collective-permute-start.61 = (bf16[32,3584]{1,0:T(8,128)(2,1)S(1)}, bf16[32,3584]{1,0:T(8,128)(2,1)S(1)}, u32[]{:S(2)}, u32[]{:S(2)}) collective-permute-start(bf16[32,3584]{1,0:T(8,128)(2,1)S(1)} %add_convert_fusion.17), channel_id=1, source_target_pairs={{0,6},{1,7},{2,4},{3,5},{4,2},{5,3},{6,0},{7,1},{8,14},{9,15},{10,... | collective-permute-start | bytes 688136 | tf_op jit(solution)/shard_map/ppermute | solution.py:119
  114.7 12.0 %collective-permute-start.59 = (bf16[32,3584]{1,0:T(8,128)(2,1)S(1)}, bf16[32,3584]{1,0:T(8,128)(2,1)S(1)}, u32[]{:S(2)}, u32[]{:S(2)}) collective-permute-start(bf16[32,3584]{1,0:T(8,128)(2,1)S(1)} %add_convert_fusion.18), channel_id=1, source_target_pairs={{0,4},{1,5},{2,6},{3,7},{4,0},{5,1},{6,2},{7,3},{8,12},{9,13},{10,... | collective-permute-start | bytes 688136 | tf_op jit(solution)/shard_map/ppermute | solution.py:119
  116.3 10.9 %collective-permute-start.57 = (bf16[32,3584]{1,0:T(8,128)(2,1)S(1)}, bf16[32,3584]{1,0:T(8,128)(2,1)S(1)}, u32[]{:S(2)}, u32[]{:S(2)}) collective-permute-start(bf16[32,3584]{1,0:T(8,128)(2,1)S(1)} %add_convert_fusion.19), channel_id=1, source_target_pairs={{0,2},{1,3},{2,0},{3,1},{4,6},{5,7},{6,4},{7,5},{8,10},{9,11},{10,... | collective-permute-start | bytes 688136 | tf_op jit(solution)/shard_map/ppermute | solution.py:119
  116.9 15.2 %collective-permute-start.64 = (bf16[32,3584]{1,0:T(8,128)(2,1)S(1)}, bf16[32,3584]{1,0:T(8,128)(2,1)S(1)}, u32[]{:S(2)}, u32[]{:S(2)}) collective-permute-start(bf16[32,3584]{1,0:T(8,128)(2,1)S(1)} %collective-permute-done.62.refs_0_), channel_id=1, source_target_pairs={{0,2},{1,3},{2,0},{3,1},{4,6},{5,7},{6,4},{7,5},{8,10},{9,11},{10,... | collective-permute-start | bytes 688136 | tf_op jit(solution)/shard_map/ppermute | solution.py:119
  118.4 13.9 %collective-permute-start.65 = (bf16[32,3584]{1,0:T(8,128)(2,1)S(1)}, bf16[32,3584]{1,0:T(8,128)(2,1)S(1)}, u32[]{:S(2)}, u32[]{:S(2)}) collective-permute-start(bf16[32,3584]{1,0:T(8,128)(2,1)S(1)} %collective-permute-done.62.refs_0_), channel_id=1, source_target_pairs={{0,4},{1,5},{2,6},{3,7},{4,0},{5,1},{6,2},{7,3},{8,12},{9,13},{10,... | collective-permute-start | bytes 688136 | tf_op jit(solution)/shard_map/ppermute | solution.py:119
  122.6 13.9 %collective-permute-start.66 = (bf16[32,3584]{1,0:T(8,128)(2,1)S(1)}, bf16[32,3584]{1,0:T(8,128)(2,1)S(1)}, u32[]{:S(2)}, u32[]{:S(2)}) collective-permute-start(bf16[32,3584]{1,0:T(8,128)(2,1)S(1)} %collective-permute-done.62.refs_0_), channel_id=1, source_target_pairs={{0,6},{1,7},{2,4},{3,5},{4,2},{5,3},{6,0},{7,1},{8,14},{9,15},{10,... | collective-permute-start | bytes 688136 | tf_op jit(solution)/shard_map/ppermute | solution.py:119
  127.4 9.2 %collective-permute-start.63 = (bf16[32,3584]{1,0:T(8,128)(2,1)S(1)}, bf16[32,3584]{1,0:T(8,128)(2,1)S(1)}, u32[]{:S(2)}, u32[]{:S(2)}) collective-permute-start(bf16[32,3584]{1,0:T(8,128)(2,1)S(1)} %add_convert_fusion.16), channel_id=1, source_target_pairs={{8,16},{16,8},{9,17},{17,9},{10,18},{18,10},{11,19},{19,11},{12,20... | collective-permute-start | bytes 688136 | tf_op jit(solution)/shard_map/ppermute | solution.py:195
  128.1 10.1 %collective-permute-start.70 = (bf16[32,3584]{1,0:T(8,128)(2,1)S(1)}, bf16[32,3584]{1,0:T(8,128)(2,1)S(1)}, u32[]{:S(2)}, u32[]{:S(2)}) collective-permute-start(bf16[32,3584]{1,0:T(8,128)(2,1)S(1)} %collective-permute-done.62.refs_0_), channel_id=1, source_target_pairs={{0,1},{1,0},{2,3},{3,2},{4,5},{5,4},{6,7},{7,6},{8,9},{9,8},{10,11... | collective-permute-start | bytes 688136 | tf_op jit(solution)/shard_map/ppermute | solution.py:119
  132.3 7.9 %collective-permute-start.72 = (bf16[32,3584]{1,0:T(8,128)(2,1)S(1)}, bf16[32,3584]{1,0:T(8,128)(2,1)S(1)}, u32[]{:S(2)}, u32[]{:S(2)}) collective-permute-start(bf16[32,3584]{1,0:T(8,128)(2,1)S(1)} %collective-permute-done.65.refs_2_), channel_id=1, source_target_pairs={{0,1},{1,0},{2,3},{3,2},{4,5},{5,4},{6,7},{7,6},{8,9},{9,8},{10,11... | collective-permute-start | bytes 688136 | tf_op jit(solution)/shard_map/ppermute | solution.py:119
  136.6 12.2 %collective-permute-start.67 = (bf16[32,3584]{1,0:T(8,128)(2,1)S(1)}, bf16[32,3584]{1,0:T(8,128)(2,1)S(1)}, u32[]{:S(2)}, u32[]{:S(2)}) collective-permute-start(bf16[32,3584]{1,0:T(8,128)(2,1)S(1)} %collective-permute-done.63.refs_0_), channel_id=1, source_target_pairs={{0,2},{1,3},{2,0},{3,1},{4,6},{5,7},{6,4},{7,5},{8,10},{9,11},{10,... | collective-permute-start | bytes 688136 | tf_op jit(solution)/shard_map/ppermute | solution.py:119
  138.2 12.6 %collective-permute-start.68 = (bf16[32,3584]{1,0:T(8,128)(2,1)S(1)}, bf16[32,3584]{1,0:T(8,128)(2,1)S(1)}, u32[]{:S(2)}, u32[]{:S(2)}) collective-permute-start(bf16[32,3584]{1,0:T(8,128)(2,1)S(1)} %collective-permute-done.63.refs_0_), channel_id=1, source_target_pairs={{0,4},{1,5},{2,6},{3,7},{4,0},{5,1},{6,2},{7,3},{8,12},{9,13},{10,... | collective-permute-start | bytes 688136 | tf_op jit(solution)/shard_map/ppermute | solution.py:119
  138.7 12.1 %collective-permute-start.69 = (bf16[32,3584]{1,0:T(8,128)(2,1)S(1)}, bf16[32,3584]{1,0:T(8,128)(2,1)S(1)}, u32[]{:S(2)}, u32[]{:S(2)}) collective-permute-start(bf16[32,3584]{1,0:T(8,128)(2,1)S(1)} %collective-permute-done.63.refs_0_), channel_id=1, source_target_pairs={{0,6},{1,7},{2,4},{3,5},{4,2},{5,3},{6,0},{7,1},{8,14},{9,15},{10,... | collective-permute-start | bytes 688136 | tf_op jit(solution)/shard_map/ppermute | solution.py:119
  155.6 12.2 %collective-permute-start.78 = (bf16[32,3584]{1,0:T(8,128)(2,1)S(1)}, bf16[32,3584]{1,0:T(8,128)(2,1)S(1)}, u32[]{:S(2)}, u32[]{:S(2)}) collective-permute-start(bf16[32,3584]{1,0:T(8,128)(2,1)S(1)} %add_convert_fusion.15), channel_id=1, source_target_pairs={{0,2},{1,3},{2,0},{3,1},{4,6},{5,7},{6,4},{7,5},{8,10},{9,11},{10,... | collective-permute-start | bytes 688136 | tf_op jit(solution)/shard_map/ppermute | solution.py:119
  156.2 12.7 %collective-permute-start.79 = (bf16[32,3584]{1,0:T(8,128)(2,1)}, bf16[32,3584]{1,0:T(8,128)(2,1)S(1)}, u32[]{:S(2)}, u32[]{:S(2)}) collective-permute-start(bf16[32,3584]{1,0:T(8,128)(2,1)} %add_convert_fusion.14), channel_id=1, source_target_pairs={{0,4},{1,5},{2,6},{3,7},{4,0},{5,1},{6,2},{7,3},{8,12},{9,13},{10,... | collective-permute-start | bytes 688136 | tf_op jit(solution)/shard_map/ppermute | solution.py:119
  157.4 11.5 %collective-permute-start.80 = (bf16[32,3584]{1,0:T(8,128)(2,1)}, bf16[32,3584]{1,0:T(8,128)(2,1)S(1)}, u32[]{:S(2)}, u32[]{:S(2)}) collective-permute-start(bf16[32,3584]{1,0:T(8,128)(2,1)} %add_convert_fusion.13), channel_id=1, source_target_pairs={{0,6},{1,7},{2,4},{3,5},{4,2},{5,3},{6,0},{7,1},{8,14},{9,15},{10,... | collective-permute-start | bytes 688136 | tf_op jit(solution)/shard_map/ppermute | solution.py:119
  169.6 7.8 %collective-permute-start.87 = (bf16[32,3584]{1,0:T(8,128)(2,1)S(1)}, bf16[32,3584]{1,0:T(8,128)(2,1)S(1)}, u32[]{:S(2)}, u32[]{:S(2)}) collective-permute-start(bf16[32,3584]{1,0:T(8,128)(2,1)S(1)} %get-tuple-element.389), channel_id=1, source_target_pairs={{0,1},{1,0},{2,3},{3,2},{4,5},{5,4},{6,7},{7,6},{8,9},{9,8},{10,11... | collective-permute-start | bytes 688136 | tf_op jit(solution)/shard_map/ppermute | solution.py:119
  169.7 11.9 %collective-permute-start.86 = (bf16[32,3584]{1,0:T(8,128)(2,1)S(1)}, bf16[32,3584]{1,0:T(8,128)(2,1)S(1)}, u32[]{:S(2)}, u32[]{:S(2)}) collective-permute-start(bf16[32,3584]{1,0:T(8,128)(2,1)S(1)} %get-tuple-element.387), channel_id=1, source_target_pairs={{0,1},{1,0},{2,3},{3,2},{4,5},{5,4},{6,7},{7,6},{8,9},{9,8},{10,11... | collective-permute-start | bytes 688136 | tf_op jit(solution)/shard_map/ppermute | solution.py:119
  170.1 9.9 %collective-permute-start.85 = (bf16[32,3584]{1,0:T(8,128)(2,1)S(1)}, bf16[32,3584]{1,0:T(8,128)(2,1)S(1)}, u32[]{:S(2)}, u32[]{:S(2)}) collective-permute-start(bf16[32,3584]{1,0:T(8,128)(2,1)S(1)} %add_convert_fusion.12), channel_id=1, source_target_pairs={{0,8},{16,24},{8,0},{24,16},{1,9},{17,25},{9,1},{25,17},{2,10},{18... | collective-permute-start | bytes 688136 | tf_op jit(solution)/shard_map/ppermute | solution.py:195
  174.3 9.5 %collective-permute-start.92 = (bf16[32,3584]{1,0:T(8,128)(2,1)S(1)}, bf16[32,3584]{1,0:T(8,128)(2,1)S(1)}, u32[]{:S(2)}, u32[]{:S(2)}) collective-permute-start(bf16[32,3584]{1,0:T(8,128)(2,1)S(1)} %add_convert_fusion.9), channel_id=1, source_target_pairs={{0,6},{1,7},{2,4},{3,5},{4,2},{5,3},{6,0},{7,1},{8,14},{9,15},{10,... | collective-permute-start | bytes 688136 | tf_op jit(solution)/shard_map/ppermute | solution.py:119
  175.9 11.7 %collective-permute-start.90 = (bf16[32,3584]{1,0:T(8,128)(2,1)S(1)}, bf16[32,3584]{1,0:T(8,128)(2,1)S(1)}, u32[]{:S(2)}, u32[]{:S(2)}) collective-permute-start(bf16[32,3584]{1,0:T(8,128)(2,1)S(1)} %add_convert_fusion.10), channel_id=1, source_target_pairs={{0,4},{1,5},{2,6},{3,7},{4,0},{5,1},{6,2},{7,3},{8,12},{9,13},{10,... | collective-permute-start | bytes 688136 | tf_op jit(solution)/shard_map/ppermute | solution.py:119
  177.5 10.9 %collective-permute-start.88 = (bf16[32,3584]{1,0:T(8,128)(2,1)S(1)}, bf16[32,3584]{1,0:T(8,128)(2,1)S(1)}, u32[]{:S(2)}, u32[]{:S(2)}) collective-permute-start(bf16[32,3584]{1,0:T(8,128)(2,1)S(1)} %add_convert_fusion.11), channel_id=1, source_target_pairs={{0,2},{1,3},{2,0},{3,1},{4,6},{5,7},{6,4},{7,5},{8,10},{9,11},{10,... | collective-permute-start | bytes 688136 | tf_op jit(solution)/shard_map/ppermute | solution.py:119
  180.1 13.3 %collective-permute-start.94 = (bf16[32,3584]{1,0:T(8,128)(2,1)S(1)}, bf16[32,3584]{1,0:T(8,128)(2,1)S(1)}, u32[]{:S(2)}, u32[]{:S(2)}) collective-permute-start(bf16[32,3584]{1,0:T(8,128)(2,1)S(1)} %collective-permute-done.85.refs_0_), channel_id=1, source_target_pairs={{0,2},{1,3},{2,0},{3,1},{4,6},{5,7},{6,4},{7,5},{8,10},{9,11},{10,... | collective-permute-start | bytes 688136 | tf_op jit(solution)/shard_map/ppermute | solution.py:119
  181.6 12.0 %collective-permute-start.95 = (bf16[32,3584]{1,0:T(8,128)(2,1)S(1)}, bf16[32,3584]{1,0:T(8,128)(2,1)S(1)}, u32[]{:S(2)}, u32[]{:S(2)}) collective-permute-start(bf16[32,3584]{1,0:T(8,128)(2,1)S(1)} %collective-permute-done.85.refs_0_), channel_id=1, source_target_pairs={{0,4},{1,5},{2,6},{3,7},{4,0},{5,1},{6,2},{7,3},{8,12},{9,13},{10,... | collective-permute-start | bytes 688136 | tf_op jit(solution)/shard_map/ppermute | solution.py:119
  183.8 13.6 %collective-permute-start.96 = (bf16[32,3584]{1,0:T(8,128)(2,1)S(1)}, bf16[32,3584]{1,0:T(8,128)(2,1)S(1)}, u32[]{:S(2)}, u32[]{:S(2)}) collective-permute-start(bf16[32,3584]{1,0:T(8,128)(2,1)S(1)} %collective-permute-done.85.refs_0_), channel_id=1, source_target_pairs={{0,6},{1,7},{2,4},{3,5},{4,2},{5,3},{6,0},{7,1},{8,14},{9,15},{10,... | collective-permute-start | bytes 688136 | tf_op jit(solution)/shard_map/ppermute | solution.py:119
  188.6 8.7 %collective-permute-start.93 = (bf16[32,3584]{1,0:T(8,128)(2,1)S(1)}, bf16[32,3584]{1,0:T(8,128)(2,1)S(1)}, u32[]{:S(2)}, u32[]{:S(2)}) collective-permute-start(bf16[32,3584]{1,0:T(8,128)(2,1)S(1)} %add_convert_fusion.8), channel_id=1, source_target_pairs={{0,8},{16,24},{8,0},{24,16},{1,9},{17,25},{9,1},{25,17},{2,10},{18... | collective-permute-start | bytes 688136 | tf_op jit(solution)/shard_map/ppermute | solution.py:195
  189.1 9.8 %collective-permute-start.100 = (bf16[32,3584]{1,0:T(8,128)(2,1)S(1)}, bf16[32,3584]{1,0:T(8,128)(2,1)S(1)}, u32[]{:S(2)}, u32[]{:S(2)}) collective-permute-start(bf16[32,3584]{1,0:T(8,128)(2,1)S(1)} %collective-permute-done.85.refs_0_), channel_id=1, source_target_pairs={{0,1},{1,0},{2,3},{3,2},{4,5},{5,4},{6,7},{7,6},{8,9},{9,8},{10,11... | collective-permute-start | bytes 688136 | tf_op jit(solution)/shard_map/ppermute | solution.py:119
  197.4 12.1 %collective-permute-start.97 = (bf16[32,3584]{1,0:T(8,128)(2,1)S(1)}, bf16[32,3584]{1,0:T(8,128)(2,1)S(1)}, u32[]{:S(2)}, u32[]{:S(2)}) collective-permute-start(bf16[32,3584]{1,0:T(8,128)(2,1)S(1)} %collective-permute-done.93.refs_0_), channel_id=1, source_target_pairs={{0,2},{1,3},{2,0},{3,1},{4,6},{5,7},{6,4},{7,5},{8,10},{9,11},{10,... | collective-permute-start | bytes 688136 | tf_op jit(solution)/shard_map/ppermute | solution.py:119
  198.9 12.7 %collective-permute-start.98 = (bf16[32,3584]{1,0:T(8,128)(2,1)S(1)}, bf16[32,3584]{1,0:T(8,128)(2,1)S(1)}, u32[]{:S(2)}, u32[]{:S(2)}) collective-permute-start(bf16[32,3584]{1,0:T(8,128)(2,1)S(1)} %collective-permute-done.93.refs_0_), channel_id=1, source_target_pairs={{0,4},{1,5},{2,6},{3,7},{4,0},{5,1},{6,2},{7,3},{8,12},{9,13},{10,... | collective-permute-start | bytes 688136 | tf_op jit(solution)/shard_map/ppermute | solution.py:119
  199.4 12.1 %collective-permute-start.99 = (bf16[32,3584]{1,0:T(8,128)(2,1)S(1)}, bf16[32,3584]{1,0:T(8,128)(2,1)S(1)}, u32[]{:S(2)}, u32[]{:S(2)}) collective-permute-start(bf16[32,3584]{1,0:T(8,128)(2,1)S(1)} %collective-permute-done.93.refs_0_), channel_id=1, source_target_pairs={{0,6},{1,7},{2,4},{3,5},{4,2},{5,3},{6,0},{7,1},{8,14},{9,15},{10,... | collective-permute-start | bytes 688136 | tf_op jit(solution)/shard_map/ppermute | solution.py:119
  215.2 12.1 %collective-permute-start.108 = (bf16[32,3584]{1,0:T(8,128)(2,1)S(1)}, bf16[32,3584]{1,0:T(8,128)(2,1)S(1)}, u32[]{:S(2)}, u32[]{:S(2)}) collective-permute-start(bf16[32,3584]{1,0:T(8,128)(2,1)S(1)} %add_convert_fusion.7), channel_id=1, source_target_pairs={{0,2},{1,3},{2,0},{3,1},{4,6},{5,7},{6,4},{7,5},{8,10},{9,11},{10,... | collective-permute-start | bytes 688136 | tf_op jit(solution)/shard_map/ppermute | solution.py:119
  215.7 12.5 %collective-permute-start.109 = (bf16[32,3584]{1,0:T(8,128)(2,1)S(1)}, bf16[32,3584]{1,0:T(8,128)(2,1)S(1)}, u32[]{:S(2)}, u32[]{:S(2)}) collective-permute-start(bf16[32,3584]{1,0:T(8,128)(2,1)S(1)} %add_convert_fusion.6), channel_id=1, source_target_pairs={{0,4},{1,5},{2,6},{3,7},{4,0},{5,1},{6,2},{7,3},{8,12},{9,13},{10,... | collective-permute-start | bytes 688136 | tf_op jit(solution)/shard_map/ppermute | solution.py:119
  216.9 11.3 %collective-permute-start.110 = (bf16[32,3584]{1,0:T(8,128)(2,1)S(1)}, bf16[32,3584]{1,0:T(8,128)(2,1)S(1)}, u32[]{:S(2)}, u32[]{:S(2)}) collective-permute-start(bf16[32,3584]{1,0:T(8,128)(2,1)S(1)} %add_convert_fusion.5), channel_id=1, source_target_pairs={{0,6},{1,7},{2,4},{3,5},{4,2},{5,3},{6,0},{7,1},{8,14},{9,15},{10,... | collective-permute-start | bytes 688136 | tf_op jit(solution)/shard_map/ppermute | solution.py:119
  230.6 9.6 %collective-permute-start.121 = (bf16[32,3584]{1,0:T(8,128)(2,1)}, bf16[32,3584]{1,0:T(8,128)(2,1)S(1)}, u32[]{:S(2)}, u32[]{:S(2)}) collective-permute-start(bf16[32,3584]{1,0:T(8,128)(2,1)} %add_convert_fusion.1), channel_id=1, source_target_pairs={{0,6},{1,7},{2,4},{3,5},{4,2},{5,3},{6,0},{7,1},{8,14},{9,15},{10,... | collective-permute-start | bytes 688136 | tf_op jit(solution)/shard_map/ppermute | solution.py:119
  232.8 11.5 %collective-permute-start.119 = (bf16[32,3584]{1,0:T(8,128)(2,1)}, bf16[32,3584]{1,0:T(8,128)(2,1)S(1)}, u32[]{:S(2)}, u32[]{:S(2)}) collective-permute-start(bf16[32,3584]{1,0:T(8,128)(2,1)} %add_convert_fusion.2), channel_id=1, source_target_pairs={{0,4},{1,5},{2,6},{3,7},{4,0},{5,1},{6,2},{7,3},{8,12},{9,13},{10,... | collective-permute-start | bytes 688136 | tf_op jit(solution)/shard_map/ppermute | solution.py:119
  235.1 9.2 %collective-permute-start.117 = (bf16[32,3584]{1,0:T(8,128)(2,1)}, bf16[32,3584]{1,0:T(8,128)(2,1)S(1)}, u32[]{:S(2)}, u32[]{:S(2)}) collective-permute-start(bf16[32,3584]{1,0:T(8,128)(2,1)} %add_convert_fusion.3), channel_id=1, source_target_pairs={{0,2},{1,3},{2,0},{3,1},{4,6},{5,7},{6,4},{7,5},{8,10},{9,11},{10,... | collective-permute-start | bytes 688136 | tf_op jit(solution)/shard_map/ppermute | solution.py:119
  (68 other events, 429.3 us)

commit v2 on v1

--- a/solution.py
+++ b/solution.py
@@ -164,14 +164,15 @@
             own = entering[m]
             if m > 0:
                 own, near[m - 1] = after(own, near[m - 1])
+            far_own = exchange(entering[m], 1)
             arrived = [exchange(own, mask) for mask in masks[1:half]]
             if m > 0:
-                arrived, outs = after(arrived, outs)
+                (arrived, far_own), outs = after((arrived, far_own), outs)
                 sums.append(on_chip(outs))
                 arrived, sums[m - 1] = after(arrived, sums[m - 1])
                 back.append(send_back(sums[m - 1]))
             near.append([entering[m]] + arrived)
-            far = [exchange(block, 1) for block in near[m]]
+            far = [far_own] + [exchange(block, 1) for block in near[m][1:]]
             outs = expert_call(
                 near[m] + far, pick[stream, m], put[stream, m], weights[stream, m], *layer
             )

time: 249 us -> 247 us (level)
  transfers between devices with their start and end apart: 122 -> 122, of which waited for: 47 -> 48; matrix products, arithmetic and copies ran while one was open for 4% -> 3% of each run, Pallas kernels for 28% -> 28%
where the time goes in v2:
time: 247 us; the launch traced here: 244 us
  starting transfers between devices  84.1 us (34%)
  waiting for transfers between devices  76.3 us (31%)
  Pallas kernels  68.7 us (28%)
  other arithmetic  10.5 us (4%)
  local copies, waits for them, and re-layouts  2.81 us (1%)
    ppermute x116, starting transfers between devices, exchange(): lax.ppermute(block, 'expert', [(i, i ^ mask) for i in range(experts)])  76.1 us
    ppermute x116, waiting for transfers between devices, exchange(): lax.ppermute(block, 'expert', [(i, i ^ mask) for i in range(experts)])  72.2 us
    pallas_call x8, Pallas kernels, expert_call(): pl.pallas_call(functools.partial(expert_kernel, count), out_shape=[jax.Sh...  68.7 us
    ppermute x6, starting transfers between devices, on_device(): entering = [lax.ppermute(block, 'pipe', pairs) for block in leaving]  7.97 us
    convert_element_type x24, other arithmetic, on_chip(): return total[:1] + [part.astype(jnp.bfloat16) for part in total[1:]]  5.53 us
  transfers between devices with their start and end apart: 122, of which 48 were waited for; matrix products, arithmetic and copies ran while one was open for 3% of the time, Pallas kernels for 28%

profile of v2, /device:TPU:0, one launch (start us, length us, event | category | flops | bytes accessed | tf_op | source)
XLA Modules:
  0.0 244.1 jit_solution(16978547330499243337)
XLA Ops:
  1.9 1.3 select_bitcast_fusion.1
  3.3 2.6 %collective-permute-start = (bf16[32,3584]{1,0:T(8,128)(2,1)S(1)}, bf16[32,3584]{1,0:T(8,128)(2,1)S(1)}, u32[]{:S(2)}, u32[]{:S(2)}) collective-permute-start(bf16[32,3584]{1,0:T(8,128)(2,1)S(1)} %get-tuple-element.462.refs_0_), channel_id=1, source_target_pairs={{0,2},{1,3},{2,0},{3,1},{4,6},{5,7},{6,4},{7,5},{8,10},{9,11},{10,... | collective-permute-start | bytes 688136 | tf_op jit(solution)/shard_map/ppermute | solution.py:119
  5.8 1.5 collective-permute-start.1
  7.5 2.0 collective-permute-start.13
  9.4 1.5 collective-permute-start.12
  10.9 3.0 %collective-permute-done.14 = f32[2,2,2,2,32,2]{4,5,3,2,1,0:T(2,128)S(1)} collective-permute-done((f32[2,2,2,2,32,2]{4,5,3,2,1,0:T(2,128)S(1)}, f32[2,2,2,2,32,2]{4,5,3,2,1,0:T(2,128)S(1)}, u32[]{:S(2)}, u32[]{:S(2)}) %collective-permute-start.14) | collective-permute-done | bytes 4128 | tf_op jit(solution)/shard_map/ppermute | solution.py:119
  13.9 1.4 collective-permute-start.2
  17.9 3.5 %collective-permute-done.2.refs_3_ = bf16[32,3584]{1,0:T(8,128)(2,1)S(1)} collective-permute-done((bf16[32,3584]{1,0:T(8,128)(2,1)S(1)}, bf16[32,3584]{1,0:T(8,128)(2,1)S(1)}, u32[]{:S(2)}, u32[]{:S(2)}) %collective-permute-start.2) | collective-permute-done | bytes 229408 | tf_op jit(solution)/shard_map/ppermute | solution.py:119
  21.5 1.6 collective-permute-start.3
  23.6 1.5 collective-permute-start.5
  25.8 8.6 %shard_map.113 = (bf16[32,3584]{1,0:T(8,128)(2,1)S(1)}, bf16[32,3584]{1,0:T(8,128)(2,1)S(1)}, bf16[32,3584]{1,0:T(8,128)(2,1)S(1)}, bf16[32,3584]{1,0:T(8,128)(2...) custom-call(bf16[32,3584]{1,0:T(8,128)(2,1)S(1)} %get-tuple-element., ...), custom_call_target="tpu_custom_call" | custom-call | flops 2818572288 | bytes 22020096 | tf_op jit(solution)/shard_map/pallas_call | solution.py:78
  34.4 1.3 collective-permute-done.4.refs_2_
  42.7 1.8 collective-permute-start.21
  44.4 8.6 %shard_map.114 = (bf16[32,3584]{1,0:T(8,128)(2,1)S(1)}, bf16[32,3584]{1,0:T(8,128)(2,1)S(1)}, bf16[32,3584]{1,0:T(8,128)(2,1)S(1)}, bf16[32,3584]{1,0:T(8,128)(2...) custom-call(bf16[32,3584]{1,0:T(8,128)(2,1)S(1)} %get-tuple-element., ...), custom_call_target="tpu_custom_call" | custom-call | flops 2818572288 | bytes 22020096 | tf_op jit(solution)/shard_map/pallas_call | solution.py:78
  55.4 1.6 collective-permute-start.25
  57.0 1.5 collective-permute-start.32
  58.6 1.6 collective-permute-start.30
  60.9 2.1 collective-permute-done.25.refs_0_
  63.0 1.5 collective-permute-start.34
  65.0 1.6 collective-permute-done.32
  66.5 1.4 collective-permute-start.36
  68.0 2.3 collective-permute-done.30
  71.9 4.2 %collective-permute-done.34.refs_1_ = bf16[32,3584]{1,0:T(8,128)(2,1)S(1)} collective-permute-done((bf16[32,3584]{1,0:T(8,128)(2,1)S(1)}, bf16[32,3584]{1,0:T(8,128)(2,1)S(1)}, u32[]{:S(2)}, u32[]{:S(2)}) %collective-permute-start.34) | collective-permute-done | bytes 229408 | tf_op jit(solution)/shard_map/ppermute | solution.py:119
  76.6 3.5 %collective-permute-done.36.refs_3_ = bf16[32,3584]{1,0:T(8,128)(2,1)S(1)} collective-permute-done((bf16[32,3584]{1,0:T(8,128)(2,1)S(1)}, bf16[32,3584]{1,0:T(8,128)(2,1)S(1)}, u32[]{:S(2)}, u32[]{:S(2)}) %collective-permute-start.36) | collective-permute-done | bytes 229408 | tf_op jit(solution)/shard_map/ppermute | solution.py:119
  80.1 1.5 collective-permute-start.37
  82.1 1.5 collective-permute-start.39
  83.6 8.6 %shard_map.115 = (bf16[32,3584]{1,0:T(8,128)(2,1)S(1)}, bf16[32,3584]{1,0:T(8,128)(2,1)S(1)}, bf16[32,3584]{1,0:T(8,128)(2,1)S(1)}, bf16[32,3584]{1,0:T(8,128)(2...) custom-call(bf16[32,3584]{1,0:T(8,128)(2,1)S(1)} %collective-permute, ...), custom_call_target="tpu_custom_call" | custom-call | flops 2818572288 | bytes 22020096 | tf_op jit(solution)/shard_map/pallas_call | solution.py:78
  92.2 2.0 collective-permute-done.38.refs_2_
  99.3 1.8 collective-permute-start.51
  101.1 8.6 %shard_map.116 = (bf16[32,3584]{1,0:T(8,128)(2,1)S(1)}, bf16[32,3584]{1,0:T(8,128)(2,1)S(1)}, bf16[32,3584]{1,0:T(8,128)(2,1)S(1)}, bf16[32,3584]{1,0:T(8,128)(2...) custom-call(bf16[32,3584]{1,0:T(8,128)(2,1)S(1)} %collective-permute, ...), custom_call_target="tpu_custom_call" | custom-call | flops 2818572288 | bytes 22020096 | tf_op jit(solution)/shard_map/pallas_call | solution.py:78
  112.6 1.5 collective-permute-start.61
  114.1 1.6 collective-permute-start.59
  116.4 1.5 collective-permute-start.64
  118.4 3.6 %collective-permute-done.61 = bf16[32,3584]{1,0:T(8,128)(2,1)S(1)} collective-permute-done((bf16[32,3584]{1,0:T(8,128)(2,1)S(1)}, bf16[32,3584]{1,0:T(8,128)(2,1)S(1)}, u32[]{:S(2)}, u32[]{:S(2)}) %collective-permute-start.61) | collective-permute-done | bytes 229408 | tf_op jit(solution)/shard_map/ppermute | solution.py:119
  122.0 1.4 collective-permute-start.66
  123.5 2.7 %collective-permute-done.59 = bf16[32,3584]{1,0:T(8,128)(2,1)S(1)} collective-permute-done((bf16[32,3584]{1,0:T(8,128)(2,1)S(1)}, bf16[32,3584]{1,0:T(8,128)(2,1)S(1)}, u32[]{:S(2)}, u32[]{:S(2)}) %collective-permute-start.59) | collective-permute-done | bytes 229408 | tf_op jit(solution)/shard_map/ppermute | solution.py:119
  127.6 4.0 %collective-permute-done.64.refs_1_ = bf16[32,3584]{1,0:T(8,128)(2,1)S(1)} collective-permute-done((bf16[32,3584]{1,0:T(8,128)(2,1)S(1)}, bf16[32,3584]{1,0:T(8,128)(2,1)S(1)}, u32[]{:S(2)}, u32[]{:S(2)}) %collective-permute-start.64) | collective-permute-done | bytes 229408 | tf_op jit(solution)/shard_map/ppermute | solution.py:119
  132.1 3.8 %collective-permute-done.66.refs_3_ = bf16[32,3584]{1,0:T(8,128)(2,1)S(1)} collective-permute-done((bf16[32,3584]{1,0:T(8,128)(2,1)S(1)}, bf16[32,3584]{1,0:T(8,128)(2,1)S(1)}, u32[]{:S(2)}, u32[]{:S(2)}) %collective-permute-start.66) | collective-permute-done | bytes 229408 | tf_op jit(solution)/shard_map/ppermute | solution.py:119
  136.1 1.6 collective-permute-start.67
  138.1 1.5 collective-permute-start.69
  139.6 8.6 %shard_map.117 = (bf16[32,3584]{1,0:T(8,128)(2,1)S(1)}, bf16[32,3584]{1,0:T(8,128)(2,1)S(1)}, bf16[32,3584]{1,0:T(8,128)(2,1)S(1)}, bf16[32,3584]{1,0:T(8,128)(2...) custom-call(bf16[32,3584]{1,0:T(8,128)(2,1)S(1)} %collective-permute, ...), custom_call_target="tpu_custom_call" | custom-call | flops 2818572288 | bytes 22020096 | tf_op jit(solution)/shard_map/pallas_call | solution.py:78
  148.3 2.0 collective-permute-done.68.refs_2_
  156.1 1.8 collective-permute-start.81
  157.9 8.6 %shard_map.118 = (bf16[32,3584]{1,0:T(8,128)(2,1)S(1)}, bf16[32,3584]{1,0:T(8,128)(2,1)S(1)}, bf16[32,3584]{1,0:T(8,128)(2,1)S(1)}, bf16[32,3584]{1,0:T(8,128)(2...) custom-call(bf16[32,3584]{1,0:T(8,128)(2,1)S(1)} %collective-permute, ...), custom_call_target="tpu_custom_call" | custom-call | flops 2818572288 | bytes 22020096 | tf_op jit(solution)/shard_map/pallas_call | solution.py:78
  168.6 4.1 %collective-permute-start.85 = (bf16[32,3584]{1,0:T(8,128)(2,1)S(1)}, bf16[32,3584]{1,0:T(8,128)(2,1)S(1)}, u32[]{:S(2)}, u32[]{:S(2)}) collective-permute-start(bf16[32,3584]{1,0:T(8,128)(2,1)S(1)} %add_convert_fusion.12), channel_id=1, source_target_pairs={{0,8},{16,24},{8,0},{24,16},{1,9},{17,25},{9,1},{25,17},{2,10},{18... | collective-permute-start | bytes 688136 | tf_op jit(solution)/shard_map/ppermute | solution.py:196
  172.8 1.5 collective-permute-start.92
  174.4 1.6 collective-permute-start.90
  176.6 2.0 collective-permute-done.85.refs_0_
  178.6 1.5 collective-permute-start.94
  180.6 1.7 collective-permute-done.92
  182.3 1.4 collective-permute-start.96
  183.8 2.3 collective-permute-done.90
  187.6 4.3 %collective-permute-done.94.refs_1_ = bf16[32,3584]{1,0:T(8,128)(2,1)S(1)} collective-permute-done((bf16[32,3584]{1,0:T(8,128)(2,1)S(1)}, bf16[32,3584]{1,0:T(8,128)(2,1)S(1)}, u32[]{:S(2)}, u32[]{:S(2)}) %collective-permute-start.94) | collective-permute-done | bytes 229408 | tf_op jit(solution)/shard_map/ppermute | solution.py:119
  192.4 3.5 %collective-permute-done.96.refs_3_ = bf16[32,3584]{1,0:T(8,128)(2,1)S(1)} collective-permute-done((bf16[32,3584]{1,0:T(8,128)(2,1)S(1)}, bf16[32,3584]{1,0:T(8,128)(2,1)S(1)}, u32[]{:S(2)}, u32[]{:S(2)}) %collective-permute-start.96) | collective-permute-done | bytes 229408 | tf_op jit(solution)/shard_map/ppermute | solution.py:119
  195.9 1.5 collective-permute-start.97
  197.9 1.5 collective-permute-start.99
  199.4 8.6 %shard_map.119 = (bf16[32,3584]{1,0:T(8,128)(2,1)S(1)}, bf16[32,3584]{1,0:T(8,128)(2,1)S(1)}, bf16[32,3584]{1,0:T(8,128)(2,1)S(1)}, bf16[32,3584]{1,0:T(8,128)(2...) custom-call(bf16[32,3584]{1,0:T(8,128)(2,1)S(1)} %collective-permute, ...), custom_call_target="tpu_custom_call" | custom-call | flops 2818572288 | bytes 22020096 | tf_op jit(solution)/shard_map/pallas_call | solution.py:78
  208.0 2.0 collective-permute-done.98.refs_2_
  215.1 1.8 collective-permute-start.111
  216.9 8.6 %shard_map.120 = (bf16[32,3584]{1,0:T(8,128)(2,1)S(1)}, bf16[32,3584]{1,0:T(8,128)(2,1)S(1)}, bf16[32,3584]{1,0:T(8,128)(2,1)S(1)}, bf16[32,3584]{1,0:T(8,128)(2...) custom-call(bf16[32,3584]{1,0:T(8,128)(2,1)S(1)} %collective-permute, ...), custom_call_target="tpu_custom_call" | custom-call | flops 2818572288 | bytes 22020096 | tf_op jit(solution)/shard_map/pallas_call | solution.py:78
  228.8 1.4 collective-permute-start.121
  231.0 1.5 collective-permute-start.119
  233.8 4.6 %collective-permute-done.121 = bf16[32,3584]{1,0:T(8,128)(2,1)S(1)} collective-permute-done((bf16[32,3584]{1,0:T(8,128)(2,1)}, bf16[32,3584]{1,0:T(8,128)(2,1)S(1)}, u32[]{:S(2)}, u32[]{:S(2)}) %collective-permute-start.121) | collective-permute-done | bytes 229408 | tf_op jit(solution)/shard_map/ppermute | solution.py:119
  238.4 4.1 %collective-permute-done.119 = bf16[32,3584]{1,0:T(8,128)(2,1)S(1)} collective-permute-done((bf16[32,3584]{1,0:T(8,128)(2,1)}, bf16[32,3584]{1,0:T(8,128)(2,1)S(1)}, u32[]{:S(2)}, u32[]{:S(2)}) %collective-permute-start.119) | collective-permute-done | bytes 229408 | tf_op jit(solution)/shard_map/ppermute | solution.py:119
  (271 shorter events, 53.6 us)
Async XLA Ops:
  3.3 14.1 %collective-permute-start = (bf16[32,3584]{1,0:T(8,128)(2,1)S(1)}, bf16[32,3584]{1,0:T(8,128)(2,1)S(1)}, u32[]{:S(2)}, u32[]{:S(2)}) collective-permute-start(bf16[32,3584]{1,0:T(8,128)(2,1)S(1)} %get-tuple-element.462.refs_0_), channel_id=1, source_target_pairs={{0,2},{1,3},{2,0},{3,1},{4,6},{5,7},{6,4},{7,5},{8,10},{9,11},{10,... | collective-permute-start | bytes 688136 | tf_op jit(solution)/shard_map/ppermute | solution.py:119
  5.8 11.7 %collective-permute-start.1 = (bf16[32,3584]{1,0:T(8,128)(2,1)S(1)}, bf16[32,3584]{1,0:T(8,128)(2,1)S(1)}, u32[]{:S(2)}, u32[]{:S(2)}) collective-permute-start(bf16[32,3584]{1,0:T(8,128)(2,1)S(1)} %get-tuple-element.462.refs_0_), channel_id=1, source_target_pairs={{0,4},{1,5},{2,6},{3,7},{4,0},{5,1},{6,2},{7,3},{8,12},{9,13},{10,... | collective-permute-start | bytes 688136 | tf_op jit(solution)/shard_map/ppermute | solution.py:119
  7.5 7.9 %collective-permute-start.13 = (f32[2,2,2,2,32,2]{4,5,3,2,1,0:T(2,128)S(1)}, f32[2,2,2,2,32,2]{4,5,3,2,1,0:T(2,128)S(1)}, u32[]{:S(2)}, u32[]{:S(2)}) collective-permute-start(f32[2,2,2,2,32,2]{4,5,3,2,1,0:T(2,128)S(1)} %get-tuple-element.473), channel_id=1, source_target_pairs={{0,4},{1,5},{2,6},{3,7},{4,0},{5,1},{6,2},{7,3},{8,12},{9,13},{10,... | collective-permute-start | bytes 12296 | tf_op jit(solution)/shard_map/ppermute | solution.py:119
  15.4 19.0 %collective-permute-start.6 = (bf16[32,3584]{1,0:T(8,128)(2,1)S(1)}, bf16[32,3584]{1,0:T(8,128)(2,1)S(1)}, u32[]{:S(2)}, u32[]{:S(2)}) collective-permute-start(bf16[32,3584]{1,0:T(8,128)(2,1)S(1)} %get-tuple-element.230.refs_0_), channel_id=1, source_target_pairs={{0,1},{1,0},{2,3},{3,2},{4,5},{5,4},{6,7},{7,6},{8,9},{9,8},{10,11... | collective-permute-start | bytes 688136 | tf_op jit(solution)/shard_map/ppermute | solution.py:119
  21.5 12.9 %collective-permute-start.3 = (bf16[32,3584]{1,0:T(8,128)(2,1)S(1)}, bf16[32,3584]{1,0:T(8,128)(2,1)S(1)}, u32[]{:S(2)}, u32[]{:S(2)}) collective-permute-start(bf16[32,3584]{1,0:T(8,128)(2,1)S(1)} %get-tuple-element.230.refs_0_), channel_id=1, source_target_pairs={{0,2},{1,3},{2,0},{3,1},{4,6},{5,7},{6,4},{7,5},{8,10},{9,11},{10,... | collective-permute-start | bytes 688136 | tf_op jit(solution)/shard_map/ppermute | solution.py:119
  23.1 12.7 %collective-permute-start.4 = (bf16[32,3584]{1,0:T(8,128)(2,1)S(1)}, bf16[32,3584]{1,0:T(8,128)(2,1)S(1)}, u32[]{:S(2)}, u32[]{:S(2)}) collective-permute-start(bf16[32,3584]{1,0:T(8,128)(2,1)S(1)} %get-tuple-element.230.refs_0_), channel_id=1, source_target_pairs={{0,4},{1,5},{2,6},{3,7},{4,0},{5,1},{6,2},{7,3},{8,12},{9,13},{10,... | collective-permute-start | bytes 688136 | tf_op jit(solution)/shard_map/ppermute | solution.py:119
  23.6 12.1 %collective-permute-start.5 = (bf16[32,3584]{1,0:T(8,128)(2,1)S(1)}, bf16[32,3584]{1,0:T(8,128)(2,1)S(1)}, u32[]{:S(2)}, u32[]{:S(2)}) collective-permute-start(bf16[32,3584]{1,0:T(8,128)(2,1)S(1)} %get-tuple-element.230.refs_0_), channel_id=1, source_target_pairs={{0,6},{1,7},{2,4},{3,5},{4,2},{5,3},{6,0},{7,1},{8,14},{9,15},{10,... | collective-permute-start | bytes 688136 | tf_op jit(solution)/shard_map/ppermute | solution.py:119
  40.9 12.2 %collective-permute-start.19 = (bf16[32,3584]{1,0:T(8,128)(2,1)S(1)}, bf16[32,3584]{1,0:T(8,128)(2,1)S(1)}, u32[]{:S(2)}, u32[]{:S(2)}) collective-permute-start(bf16[32,3584]{1,0:T(8,128)(2,1)S(1)} %add_convert_fusion.31), channel_id=1, source_target_pairs={{0,2},{1,3},{2,0},{3,1},{4,6},{5,7},{6,4},{7,5},{8,10},{9,11},{10,... | collective-permute-start | bytes 688136 | tf_op jit(solution)/shard_map/ppermute | solution.py:119
  41.5 12.7 %collective-permute-start.20 = (bf16[32,3584]{1,0:T(8,128)(2,1)}, bf16[32,3584]{1,0:T(8,128)(2,1)S(1)}, u32[]{:S(2)}, u32[]{:S(2)}) collective-permute-start(bf16[32,3584]{1,0:T(8,128)(2,1)} %add_convert_fusion.30), channel_id=1, source_target_pairs={{0,4},{1,5},{2,6},{3,7},{4,0},{5,1},{6,2},{7,3},{8,12},{9,13},{10,... | collective-permute-start | bytes 688136 | tf_op jit(solution)/shard_map/ppermute | solution.py:119
  42.7 11.5 %collective-permute-start.21 = (bf16[32,3584]{1,0:T(8,128)(2,1)}, bf16[32,3584]{1,0:T(8,128)(2,1)S(1)}, u32[]{:S(2)}, u32[]{:S(2)}) collective-permute-start(bf16[32,3584]{1,0:T(8,128)(2,1)} %add_convert_fusion.29), channel_id=1, source_target_pairs={{0,6},{1,7},{2,4},{3,5},{4,2},{5,3},{6,0},{7,1},{8,14},{9,15},{10,... | collective-permute-start | bytes 688136 | tf_op jit(solution)/shard_map/ppermute | solution.py:119
  55.0 9.5 %collective-permute-start.26 = (bf16[32,3584]{1,0:T(8,128)(2,1)S(1)}, bf16[32,3584]{1,0:T(8,128)(2,1)S(1)}, u32[]{:S(2)}, u32[]{:S(2)}) collective-permute-start(bf16[32,3584]{1,0:T(8,128)(2,1)S(1)} %get-tuple-element.280), channel_id=1, source_target_pairs={{0,1},{1,0},{2,3},{3,2},{4,5},{5,4},{6,7},{7,6},{8,9},{9,8},{10,11... | collective-permute-start | bytes 688136 | tf_op jit(solution)/shard_map/ppermute | solution.py:119
  55.4 7.6 %collective-permute-start.25 = (bf16[32,3584]{1,0:T(8,128)(2,1)S(1)}, bf16[32,3584]{1,0:T(8,128)(2,1)S(1)}, u32[]{:S(2)}, u32[]{:S(2)}) collective-permute-start(bf16[32,3584]{1,0:T(8,128)(2,1)S(1)} %add_convert_fusion.28), channel_id=1, source_target_pairs={{0,8},{16,24},{8,0},{24,16},{1,9},{17,25},{9,1},{25,17},{2,10},{18... | collective-permute-start | bytes 688136 | tf_op jit(solution)/shard_map/ppermute | solution.py:196
  57.0 9.5 %collective-permute-start.32 = (bf16[32,3584]{1,0:T(8,128)(2,1)S(1)}, bf16[32,3584]{1,0:T(8,128)(2,1)S(1)}, u32[]{:S(2)}, u32[]{:S(2)}) collective-permute-start(bf16[32,3584]{1,0:T(8,128)(2,1)S(1)} %add_convert_fusion.25), channel_id=1, source_target_pairs={{0,6},{1,7},{2,4},{3,5},{4,2},{5,3},{6,0},{7,1},{8,14},{9,15},{10,... | collective-permute-start | bytes 688136 | tf_op jit(solution)/shard_map/ppermute | solution.py:119
  58.6 11.7 %collective-permute-start.30 = (bf16[32,3584]{1,0:T(8,128)(2,1)S(1)}, bf16[32,3584]{1,0:T(8,128)(2,1)S(1)}, u32[]{:S(2)}, u32[]{:S(2)}) collective-permute-start(bf16[32,3584]{1,0:T(8,128)(2,1)S(1)} %add_convert_fusion.26), channel_id=1, source_target_pairs={{0,4},{1,5},{2,6},{3,7},{4,0},{5,1},{6,2},{7,3},{8,12},{9,13},{10,... | collective-permute-start | bytes 688136 | tf_op jit(solution)/shard_map/ppermute | solution.py:119
  60.2 10.9 %collective-permute-start.28 = (bf16[32,3584]{1,0:T(8,128)(2,1)S(1)}, bf16[32,3584]{1,0:T(8,128)(2,1)S(1)}, u32[]{:S(2)}, u32[]{:S(2)}) collective-permute-start(bf16[32,3584]{1,0:T(8,128)(2,1)S(1)} %add_convert_fusion.27), channel_id=1, source_target_pairs={{0,2},{1,3},{2,0},{3,1},{4,6},{5,7},{6,4},{7,5},{8,10},{9,11},{10,... | collective-permute-start | bytes 688136 | tf_op jit(solution)/shard_map/ppermute | solution.py:119
  63.0 13.1 %collective-permute-start.34 = (bf16[32,3584]{1,0:T(8,128)(2,1)S(1)}, bf16[32,3584]{1,0:T(8,128)(2,1)S(1)}, u32[]{:S(2)}, u32[]{:S(2)}) collective-permute-start(bf16[32,3584]{1,0:T(8,128)(2,1)S(1)} %collective-permute-done.25.refs_0_), channel_id=1, source_target_pairs={{0,2},{1,3},{2,0},{3,1},{4,6},{5,7},{6,4},{7,5},{8,10},{9,11},{10,... | collective-permute-start | bytes 688136 | tf_op jit(solution)/shard_map/ppermute | solution.py:119
  64.5 11.8 %collective-permute-start.35 = (bf16[32,3584]{1,0:T(8,128)(2,1)S(1)}, bf16[32,3584]{1,0:T(8,128)(2,1)S(1)}, u32[]{:S(2)}, u32[]{:S(2)}) collective-permute-start(bf16[32,3584]{1,0:T(8,128)(2,1)S(1)} %collective-permute-done.25.refs_0_), channel_id=1, source_target_pairs={{0,4},{1,5},{2,6},{3,7},{4,0},{5,1},{6,2},{7,3},{8,12},{9,13},{10,... | collective-permute-start | bytes 688136 | tf_op jit(solution)/shard_map/ppermute | solution.py:119
  66.5 13.6 %collective-permute-start.36 = (bf16[32,3584]{1,0:T(8,128)(2,1)S(1)}, bf16[32,3584]{1,0:T(8,128)(2,1)S(1)}, u32[]{:S(2)}, u32[]{:S(2)}) collective-permute-start(bf16[32,3584]{1,0:T(8,128)(2,1)S(1)} %collective-permute-done.25.refs_0_), channel_id=1, source_target_pairs={{0,6},{1,7},{2,4},{3,5},{4,2},{5,3},{6,0},{7,1},{8,14},{9,15},{10,... | collective-permute-start | bytes 688136 | tf_op jit(solution)/shard_map/ppermute | solution.py:119
  71.4 8.7 %collective-permute-start.33 = (bf16[32,3584]{1,0:T(8,128)(2,1)S(1)}, bf16[32,3584]{1,0:T(8,128)(2,1)S(1)}, u32[]{:S(2)}, u32[]{:S(2)}) collective-permute-start(bf16[32,3584]{1,0:T(8,128)(2,1)S(1)} %add_convert_fusion.24), channel_id=1, source_target_pairs={{0,8},{16,24},{8,0},{24,16},{1,9},{17,25},{9,1},{25,17},{2,10},{18... | collective-permute-start | bytes 688136 | tf_op jit(solution)/shard_map/ppermute | solution.py:196
  71.9 9.7 %collective-permute-start.41 = (bf16[32,3584]{1,0:T(8,128)(2,1)S(1)}, bf16[32,3584]{1,0:T(8,128)(2,1)S(1)}, u32[]{:S(2)}, u32[]{:S(2)}) collective-permute-start(bf16[32,3584]{1,0:T(8,128)(2,1)S(1)} %collective-permute-done.25.refs_0_), channel_id=1, source_target_pairs={{0,1},{1,0},{2,3},{3,2},{4,5},{5,4},{6,7},{7,6},{8,9},{9,8},{10,11... | collective-permute-start | bytes 688136 | tf_op jit(solution)/shard_map/ppermute | solution.py:119
  80.1 12.1 %collective-permute-start.37 = (bf16[32,3584]{1,0:T(8,128)(2,1)S(1)}, bf16[32,3584]{1,0:T(8,128)(2,1)S(1)}, u32[]{:S(2)}, u32[]{:S(2)}) collective-permute-start(bf16[32,3584]{1,0:T(8,128)(2,1)S(1)} %collective-permute-done.33.refs_0_), channel_id=1, source_target_pairs={{0,2},{1,3},{2,0},{3,1},{4,6},{5,7},{6,4},{7,5},{8,10},{9,11},{10,... | collective-permute-start | bytes 688136 | tf_op jit(solution)/shard_map/ppermute | solution.py:119
  81.6 12.7 %collective-permute-start.38 = (bf16[32,3584]{1,0:T(8,128)(2,1)S(1)}, bf16[32,3584]{1,0:T(8,128)(2,1)S(1)}, u32[]{:S(2)}, u32[]{:S(2)}) collective-permute-start(bf16[32,3584]{1,0:T(8,128)(2,1)S(1)} %collective-permute-done.33.refs_0_), channel_id=1, source_target_pairs={{0,4},{1,5},{2,6},{3,7},{4,0},{5,1},{6,2},{7,3},{8,12},{9,13},{10,... | collective-permute-start | bytes 688136 | tf_op jit(solution)/shard_map/ppermute | solution.py:119
  82.1 12.1 %collective-permute-start.39 = (bf16[32,3584]{1,0:T(8,128)(2,1)S(1)}, bf16[32,3584]{1,0:T(8,128)(2,1)S(1)}, u32[]{:S(2)}, u32[]{:S(2)}) collective-permute-start(bf16[32,3584]{1,0:T(8,128)(2,1)S(1)} %collective-permute-done.33.refs_0_), channel_id=1, source_target_pairs={{0,6},{1,7},{2,4},{3,5},{4,2},{5,3},{6,0},{7,1},{8,14},{9,15},{10,... | collective-permute-start | bytes 688136 | tf_op jit(solution)/shard_map/ppermute | solution.py:119
  83.6 10.6 %collective-permute-start.40 = (bf16[32,3584]{1,0:T(8,128)(2,1)S(1)}, bf16[32,3584]{1,0:T(8,128)(2,1)S(1)}, u32[]{:S(2)}, u32[]{:S(2)}) collective-permute-start(bf16[32,3584]{1,0:T(8,128)(2,1)S(1)} %collective-permute-done.33.refs_0_), channel_id=1, source_target_pairs={{0,1},{1,0},{2,3},{3,2},{4,5},{5,4},{6,7},{7,6},{8,9},{9,8},{10,11... | collective-permute-start | bytes 688136 | tf_op jit(solution)/shard_map/ppermute | solution.py:119
  97.6 12.1 %collective-permute-start.49 = (bf16[32,3584]{1,0:T(8,128)(2,1)S(1)}, bf16[32,3584]{1,0:T(8,128)(2,1)S(1)}, u32[]{:S(2)}, u32[]{:S(2)}) collective-permute-start(bf16[32,3584]{1,0:T(8,128)(2,1)S(1)} %add_convert_fusion.23), channel_id=1, source_target_pairs={{0,2},{1,3},{2,0},{3,1},{4,6},{5,7},{6,4},{7,5},{8,10},{9,11},{10,... | collective-permute-start | bytes 688136 | tf_op jit(solution)/shard_map/ppermute | solution.py:119
  98.1 12.5 %collective-permute-start.50 = (bf16[32,3584]{1,0:T(8,128)(2,1)S(1)}, bf16[32,3584]{1,0:T(8,128)(2,1)S(1)}, u32[]{:S(2)}, u32[]{:S(2)}) collective-permute-start(bf16[32,3584]{1,0:T(8,128)(2,1)S(1)} %add_convert_fusion.22), channel_id=1, source_target_pairs={{0,4},{1,5},{2,6},{3,7},{4,0},{5,1},{6,2},{7,3},{8,12},{9,13},{10,... | collective-permute-start | bytes 688136 | tf_op jit(solution)/shard_map/ppermute | solution.py:119
  99.3 11.3 %collective-permute-start.51 = (bf16[32,3584]{1,0:T(8,128)(2,1)S(1)}, bf16[32,3584]{1,0:T(8,128)(2,1)S(1)}, u32[]{:S(2)}, u32[]{:S(2)}) collective-permute-start(bf16[32,3584]{1,0:T(8,128)(2,1)S(1)} %add_convert_fusion.21), channel_id=1, source_target_pairs={{0,6},{1,7},{2,4},{3,5},{4,2},{5,3},{6,0},{7,1},{8,14},{9,15},{10,... | collective-permute-start | bytes 688136 | tf_op jit(solution)/shard_map/ppermute | solution.py:119
  112.6 9.5 %collective-permute-start.61 = (bf16[32,3584]{1,0:T(8,128)(2,1)S(1)}, bf16[32,3584]{1,0:T(8,128)(2,1)S(1)}, u32[]{:S(2)}, u32[]{:S(2)}) collective-permute-start(bf16[32,3584]{1,0:T(8,128)(2,1)S(1)} %add_convert_fusion.17), channel_id=1, source_target_pairs={{0,6},{1,7},{2,4},{3,5},{4,2},{5,3},{6,0},{7,1},{8,14},{9,15},{10,... | collective-permute-start | bytes 688136 | tf_op jit(solution)/shard_map/ppermute | solution.py:119
  114.1 12.0 %collective-permute-start.59 = (bf16[32,3584]{1,0:T(8,128)(2,1)S(1)}, bf16[32,3584]{1,0:T(8,128)(2,1)S(1)}, u32[]{:S(2)}, u32[]{:S(2)}) collective-permute-start(bf16[32,3584]{1,0:T(8,128)(2,1)S(1)} %add_convert_fusion.18), channel_id=1, source_target_pairs={{0,4},{1,5},{2,6},{3,7},{4,0},{5,1},{6,2},{7,3},{8,12},{9,13},{10,... | collective-permute-start | bytes 688136 | tf_op jit(solution)/shard_map/ppermute | solution.py:119
  115.8 10.9 %collective-permute-start.57 = (bf16[32,3584]{1,0:T(8,128)(2,1)S(1)}, bf16[32,3584]{1,0:T(8,128)(2,1)S(1)}, u32[]{:S(2)}, u32[]{:S(2)}) collective-permute-start(bf16[32,3584]{1,0:T(8,128)(2,1)S(1)} %add_convert_fusion.19), channel_id=1, source_target_pairs={{0,2},{1,3},{2,0},{3,1},{4,6},{5,7},{6,4},{7,5},{8,10},{9,11},{10,... | collective-permute-start | bytes 688136 | tf_op jit(solution)/shard_map/ppermute | solution.py:119
  116.4 15.2 %collective-permute-start.64 = (bf16[32,3584]{1,0:T(8,128)(2,1)S(1)}, bf16[32,3584]{1,0:T(8,128)(2,1)S(1)}, u32[]{:S(2)}, u32[]{:S(2)}) collective-permute-start(bf16[32,3584]{1,0:T(8,128)(2,1)S(1)} %collective-permute-done.62.refs_0_), channel_id=1, source_target_pairs={{0,2},{1,3},{2,0},{3,1},{4,6},{5,7},{6,4},{7,5},{8,10},{9,11},{10,... | collective-permute-start | bytes 688136 | tf_op jit(solution)/shard_map/ppermute | solution.py:119
  117.9 13.9 %collective-permute-start.65 = (bf16[32,3584]{1,0:T(8,128)(2,1)S(1)}, bf16[32,3584]{1,0:T(8,128)(2,1)S(1)}, u32[]{:S(2)}, u32[]{:S(2)}) collective-permute-start(bf16[32,3584]{1,0:T(8,128)(2,1)S(1)} %collective-permute-done.62.refs_0_), channel_id=1, source_target_pairs={{0,4},{1,5},{2,6},{3,7},{4,0},{5,1},{6,2},{7,3},{8,12},{9,13},{10,... | collective-permute-start | bytes 688136 | tf_op jit(solution)/shard_map/ppermute | solution.py:119
  122.0 13.9 %collective-permute-start.66 = (bf16[32,3584]{1,0:T(8,128)(2,1)S(1)}, bf16[32,3584]{1,0:T(8,128)(2,1)S(1)}, u32[]{:S(2)}, u32[]{:S(2)}) collective-permute-start(bf16[32,3584]{1,0:T(8,128)(2,1)S(1)} %collective-permute-done.62.refs_0_), channel_id=1, source_target_pairs={{0,6},{1,7},{2,4},{3,5},{4,2},{5,3},{6,0},{7,1},{8,14},{9,15},{10,... | collective-permute-start | bytes 688136 | tf_op jit(solution)/shard_map/ppermute | solution.py:119
  126.9 9.2 %collective-permute-start.63 = (bf16[32,3584]{1,0:T(8,128)(2,1)S(1)}, bf16[32,3584]{1,0:T(8,128)(2,1)S(1)}, u32[]{:S(2)}, u32[]{:S(2)}) collective-permute-start(bf16[32,3584]{1,0:T(8,128)(2,1)S(1)} %add_convert_fusion.16), channel_id=1, source_target_pairs={{8,16},{16,8},{9,17},{17,9},{10,18},{18,10},{11,19},{19,11},{12,20... | collective-permute-start | bytes 688136 | tf_op jit(solution)/shard_map/ppermute | solution.py:196
  127.5 10.1 %collective-permute-start.71 = (bf16[32,3584]{1,0:T(8,128)(2,1)S(1)}, bf16[32,3584]{1,0:T(8,128)(2,1)S(1)}, u32[]{:S(2)}, u32[]{:S(2)}) collective-permute-start(bf16[32,3584]{1,0:T(8,128)(2,1)S(1)} %collective-permute-done.62.refs_0_), channel_id=1, source_target_pairs={{0,1},{1,0},{2,3},{3,2},{4,5},{5,4},{6,7},{7,6},{8,9},{9,8},{10,11... | collective-permute-start | bytes 688136 | tf_op jit(solution)/shard_map/ppermute | solution.py:119
  131.8 7.9 %collective-permute-start.73 = (bf16[32,3584]{1,0:T(8,128)(2,1)S(1)}, bf16[32,3584]{1,0:T(8,128)(2,1)S(1)}, u32[]{:S(2)}, u32[]{:S(2)}) collective-permute-start(bf16[32,3584]{1,0:T(8,128)(2,1)S(1)} %collective-permute-done.65.refs_2_), channel_id=1, source_target_pairs={{0,1},{1,0},{2,3},{3,2},{4,5},{5,4},{6,7},{7,6},{8,9},{9,8},{10,11... | collective-permute-start | bytes 688136 | tf_op jit(solution)/shard_map/ppermute | solution.py:119
  136.1 12.2 %collective-permute-start.67 = (bf16[32,3584]{1,0:T(8,128)(2,1)S(1)}, bf16[32,3584]{1,0:T(8,128)(2,1)S(1)}, u32[]{:S(2)}, u32[]{:S(2)}) collective-permute-start(bf16[32,3584]{1,0:T(8,128)(2,1)S(1)} %collective-permute-done.63.refs_0_), channel_id=1, source_target_pairs={{0,2},{1,3},{2,0},{3,1},{4,6},{5,7},{6,4},{7,5},{8,10},{9,11},{10,... | collective-permute-start | bytes 688136 | tf_op jit(solution)/shard_map/ppermute | solution.py:119
  137.6 12.6 %collective-permute-start.68 = (bf16[32,3584]{1,0:T(8,128)(2,1)S(1)}, bf16[32,3584]{1,0:T(8,128)(2,1)S(1)}, u32[]{:S(2)}, u32[]{:S(2)}) collective-permute-start(bf16[32,3584]{1,0:T(8,128)(2,1)S(1)} %collective-permute-done.63.refs_0_), channel_id=1, source_target_pairs={{0,4},{1,5},{2,6},{3,7},{4,0},{5,1},{6,2},{7,3},{8,12},{9,13},{10,... | collective-permute-start | bytes 688136 | tf_op jit(solution)/shard_map/ppermute | solution.py:119
  138.1 12.1 %collective-permute-start.69 = (bf16[32,3584]{1,0:T(8,128)(2,1)S(1)}, bf16[32,3584]{1,0:T(8,128)(2,1)S(1)}, u32[]{:S(2)}, u32[]{:S(2)}) collective-permute-start(bf16[32,3584]{1,0:T(8,128)(2,1)S(1)} %collective-permute-done.63.refs_0_), channel_id=1, source_target_pairs={{0,6},{1,7},{2,4},{3,5},{4,2},{5,3},{6,0},{7,1},{8,14},{9,15},{10,... | collective-permute-start | bytes 688136 | tf_op jit(solution)/shard_map/ppermute | solution.py:119
  139.6 10.6 %collective-permute-start.70 = (bf16[32,3584]{1,0:T(8,128)(2,1)S(1)}, bf16[32,3584]{1,0:T(8,128)(2,1)S(1)}, u32[]{:S(2)}, u32[]{:S(2)}) collective-permute-start(bf16[32,3584]{1,0:T(8,128)(2,1)S(1)} %collective-permute-done.63.refs_0_), channel_id=1, source_target_pairs={{0,1},{1,0},{2,3},{3,2},{4,5},{5,4},{6,7},{7,6},{8,9},{9,8},{10,11... | collective-permute-start | bytes 688136 | tf_op jit(solution)/shard_map/ppermute | solution.py:119
  154.3 12.2 %collective-permute-start.79 = (bf16[32,3584]{1,0:T(8,128)(2,1)S(1)}, bf16[32,3584]{1,0:T(8,128)(2,1)S(1)}, u32[]{:S(2)}, u32[]{:S(2)}) collective-permute-start(bf16[32,3584]{1,0:T(8,128)(2,1)S(1)} %add_convert_fusion.15), channel_id=1, source_target_pairs={{0,2},{1,3},{2,0},{3,1},{4,6},{5,7},{6,4},{7,5},{8,10},{9,11},{10,... | collective-permute-start | bytes 688136 | tf_op jit(solution)/shard_map/ppermute | solution.py:119
  154.9 12.5 %collective-permute-start.80 = (bf16[32,3584]{1,0:T(8,128)(2,1)S(1)}, bf16[32,3584]{1,0:T(8,128)(2,1)S(1)}, u32[]{:S(2)}, u32[]{:S(2)}) collective-permute-start(bf16[32,3584]{1,0:T(8,128)(2,1)S(1)} %add_convert_fusion.14), channel_id=1, source_target_pairs={{0,4},{1,5},{2,6},{3,7},{4,0},{5,1},{6,2},{7,3},{8,12},{9,13},{10,... | collective-permute-start | bytes 688136 | tf_op jit(solution)/shard_map/ppermute | solution.py:119
  156.1 11.3 %collective-permute-start.81 = (bf16[32,3584]{1,0:T(8,128)(2,1)}, bf16[32,3584]{1,0:T(8,128)(2,1)S(1)}, u32[]{:S(2)}, u32[]{:S(2)}) collective-permute-start(bf16[32,3584]{1,0:T(8,128)(2,1)} %add_convert_fusion.13), channel_id=1, source_target_pairs={{0,6},{1,7},{2,4},{3,5},{4,2},{5,3},{6,0},{7,1},{8,14},{9,15},{10,... | collective-permute-start | bytes 688136 | tf_op jit(solution)/shard_map/ppermute | solution.py:119
  168.1 7.8 %collective-permute-start.87 = (bf16[32,3584]{1,0:T(8,128)(2,1)S(1)}, bf16[32,3584]{1,0:T(8,128)(2,1)S(1)}, u32[]{:S(2)}, u32[]{:S(2)}) collective-permute-start(bf16[32,3584]{1,0:T(8,128)(2,1)S(1)} %get-tuple-element.396), channel_id=1, source_target_pairs={{0,1},{1,0},{2,3},{3,2},{4,5},{5,4},{6,7},{7,6},{8,9},{9,8},{10,11... | collective-permute-start | bytes 688136 | tf_op jit(solution)/shard_map/ppermute | solution.py:119
  168.2 11.9 %collective-permute-start.86 = (bf16[32,3584]{1,0:T(8,128)(2,1)S(1)}, bf16[32,3584]{1,0:T(8,128)(2,1)S(1)}, u32[]{:S(2)}, u32[]{:S(2)}) collective-permute-start(bf16[32,3584]{1,0:T(8,128)(2,1)S(1)} %get-tuple-element.394), channel_id=1, source_target_pairs={{0,1},{1,0},{2,3},{3,2},{4,5},{5,4},{6,7},{7,6},{8,9},{9,8},{10,11... | collective-permute-start | bytes 688136 | tf_op jit(solution)/shard_map/ppermute | solution.py:119
  168.6 9.9 %collective-permute-start.85 = (bf16[32,3584]{1,0:T(8,128)(2,1)S(1)}, bf16[32,3584]{1,0:T(8,128)(2,1)S(1)}, u32[]{:S(2)}, u32[]{:S(2)}) collective-permute-start(bf16[32,3584]{1,0:T(8,128)(2,1)S(1)} %add_convert_fusion.12), channel_id=1, source_target_pairs={{0,8},{16,24},{8,0},{24,16},{1,9},{17,25},{9,1},{25,17},{2,10},{18... | collective-permute-start | bytes 688136 | tf_op jit(solution)/shard_map/ppermute | solution.py:196
  172.8 9.5 %collective-permute-start.92 = (bf16[32,3584]{1,0:T(8,128)(2,1)S(1)}, bf16[32,3584]{1,0:T(8,128)(2,1)S(1)}, u32[]{:S(2)}, u32[]{:S(2)}) collective-permute-start(bf16[32,3584]{1,0:T(8,128)(2,1)S(1)} %add_convert_fusion.9), channel_id=1, source_target_pairs={{0,6},{1,7},{2,4},{3,5},{4,2},{5,3},{6,0},{7,1},{8,14},{9,15},{10,... | collective-permute-start | bytes 688136 | tf_op jit(solution)/shard_map/ppermute | solution.py:119
  174.4 11.7 %collective-permute-start.90 = (bf16[32,3584]{1,0:T(8,128)(2,1)S(1)}, bf16[32,3584]{1,0:T(8,128)(2,1)S(1)}, u32[]{:S(2)}, u32[]{:S(2)}) collective-permute-start(bf16[32,3584]{1,0:T(8,128)(2,1)S(1)} %add_convert_fusion.10), channel_id=1, source_target_pairs={{0,4},{1,5},{2,6},{3,7},{4,0},{5,1},{6,2},{7,3},{8,12},{9,13},{10,... | collective-permute-start | bytes 688136 | tf_op jit(solution)/shard_map/ppermute | solution.py:119
  176.0 10.9 %collective-permute-start.88 = (bf16[32,3584]{1,0:T(8,128)(2,1)S(1)}, bf16[32,3584]{1,0:T(8,128)(2,1)S(1)}, u32[]{:S(2)}, u32[]{:S(2)}) collective-permute-start(bf16[32,3584]{1,0:T(8,128)(2,1)S(1)} %add_convert_fusion.11), channel_id=1, source_target_pairs={{0,2},{1,3},{2,0},{3,1},{4,6},{5,7},{6,4},{7,5},{8,10},{9,11},{10,... | collective-permute-start | bytes 688136 | tf_op jit(solution)/shard_map/ppermute | solution.py:119
  178.6 13.3 %collective-permute-start.94 = (bf16[32,3584]{1,0:T(8,128)(2,1)S(1)}, bf16[32,3584]{1,0:T(8,128)(2,1)S(1)}, u32[]{:S(2)}, u32[]{:S(2)}) collective-permute-start(bf16[32,3584]{1,0:T(8,128)(2,1)S(1)} %collective-permute-done.85.refs_0_), channel_id=1, source_target_pairs={{0,2},{1,3},{2,0},{3,1},{4,6},{5,7},{6,4},{7,5},{8,10},{9,11},{10,... | collective-permute-start | bytes 688136 | tf_op jit(solution)/shard_map/ppermute | solution.py:119
  180.1 12.0 %collective-permute-start.95 = (bf16[32,3584]{1,0:T(8,128)(2,1)S(1)}, bf16[32,3584]{1,0:T(8,128)(2,1)S(1)}, u32[]{:S(2)}, u32[]{:S(2)}) collective-permute-start(bf16[32,3584]{1,0:T(8,128)(2,1)S(1)} %collective-permute-done.85.refs_0_), channel_id=1, source_target_pairs={{0,4},{1,5},{2,6},{3,7},{4,0},{5,1},{6,2},{7,3},{8,12},{9,13},{10,... | collective-permute-start | bytes 688136 | tf_op jit(solution)/shard_map/ppermute | solution.py:119
  182.3 13.6 %collective-permute-start.96 = (bf16[32,3584]{1,0:T(8,128)(2,1)S(1)}, bf16[32,3584]{1,0:T(8,128)(2,1)S(1)}, u32[]{:S(2)}, u32[]{:S(2)}) collective-permute-start(bf16[32,3584]{1,0:T(8,128)(2,1)S(1)} %collective-permute-done.85.refs_0_), channel_id=1, source_target_pairs={{0,6},{1,7},{2,4},{3,5},{4,2},{5,3},{6,0},{7,1},{8,14},{9,15},{10,... | collective-permute-start | bytes 688136 | tf_op jit(solution)/shard_map/ppermute | solution.py:119
  187.1 8.7 %collective-permute-start.93 = (bf16[32,3584]{1,0:T(8,128)(2,1)S(1)}, bf16[32,3584]{1,0:T(8,128)(2,1)S(1)}, u32[]{:S(2)}, u32[]{:S(2)}) collective-permute-start(bf16[32,3584]{1,0:T(8,128)(2,1)S(1)} %add_convert_fusion.8), channel_id=1, source_target_pairs={{0,8},{16,24},{8,0},{24,16},{1,9},{17,25},{9,1},{25,17},{2,10},{18... | collective-permute-start | bytes 688136 | tf_op jit(solution)/shard_map/ppermute | solution.py:196
  187.6 9.7 %collective-permute-start.101 = (bf16[32,3584]{1,0:T(8,128)(2,1)S(1)}, bf16[32,3584]{1,0:T(8,128)(2,1)S(1)}, u32[]{:S(2)}, u32[]{:S(2)}) collective-permute-start(bf16[32,3584]{1,0:T(8,128)(2,1)S(1)} %collective-permute-done.85.refs_0_), channel_id=1, source_target_pairs={{0,1},{1,0},{2,3},{3,2},{4,5},{5,4},{6,7},{7,6},{8,9},{9,8},{10,11... | collective-permute-start | bytes 688136 | tf_op jit(solution)/shard_map/ppermute | solution.py:119
  195.9 12.1 %collective-permute-start.97 = (bf16[32,3584]{1,0:T(8,128)(2,1)S(1)}, bf16[32,3584]{1,0:T(8,128)(2,1)S(1)}, u32[]{:S(2)}, u32[]{:S(2)}) collective-permute-start(bf16[32,3584]{1,0:T(8,128)(2,1)S(1)} %collective-permute-done.93.refs_0_), channel_id=1, source_target_pairs={{0,2},{1,3},{2,0},{3,1},{4,6},{5,7},{6,4},{7,5},{8,10},{9,11},{10,... | collective-permute-start | bytes 688136 | tf_op jit(solution)/shard_map/ppermute | solution.py:119
  197.4 12.7 %collective-permute-start.98 = (bf16[32,3584]{1,0:T(8,128)(2,1)S(1)}, bf16[32,3584]{1,0:T(8,128)(2,1)S(1)}, u32[]{:S(2)}, u32[]{:S(2)}) collective-permute-start(bf16[32,3584]{1,0:T(8,128)(2,1)S(1)} %collective-permute-done.93.refs_0_), channel_id=1, source_target_pairs={{0,4},{1,5},{2,6},{3,7},{4,0},{5,1},{6,2},{7,3},{8,12},{9,13},{10,... | collective-permute-start | bytes 688136 | tf_op jit(solution)/shard_map/ppermute | solution.py:119
  197.9 12.1 %collective-permute-start.99 = (bf16[32,3584]{1,0:T(8,128)(2,1)S(1)}, bf16[32,3584]{1,0:T(8,128)(2,1)S(1)}, u32[]{:S(2)}, u32[]{:S(2)}) collective-permute-start(bf16[32,3584]{1,0:T(8,128)(2,1)S(1)} %collective-permute-done.93.refs_0_), channel_id=1, source_target_pairs={{0,6},{1,7},{2,4},{3,5},{4,2},{5,3},{6,0},{7,1},{8,14},{9,15},{10,... | collective-permute-start | bytes 688136 | tf_op jit(solution)/shard_map/ppermute | solution.py:119
  199.4 10.6 %collective-permute-start.100 = (bf16[32,3584]{1,0:T(8,128)(2,1)S(1)}, bf16[32,3584]{1,0:T(8,128)(2,1)S(1)}, u32[]{:S(2)}, u32[]{:S(2)}) collective-permute-start(bf16[32,3584]{1,0:T(8,128)(2,1)S(1)} %collective-permute-done.93.refs_0_), channel_id=1, source_target_pairs={{0,1},{1,0},{2,3},{3,2},{4,5},{5,4},{6,7},{7,6},{8,9},{9,8},{10,11... | collective-permute-start | bytes 688136 | tf_op jit(solution)/shard_map/ppermute | solution.py:119
  213.4 12.1 %collective-permute-start.109 = (bf16[32,3584]{1,0:T(8,128)(2,1)S(1)}, bf16[32,3584]{1,0:T(8,128)(2,1)S(1)}, u32[]{:S(2)}, u32[]{:S(2)}) collective-permute-start(bf16[32,3584]{1,0:T(8,128)(2,1)S(1)} %add_convert_fusion.7), channel_id=1, source_target_pairs={{0,2},{1,3},{2,0},{3,1},{4,6},{5,7},{6,4},{7,5},{8,10},{9,11},{10,... | collective-permute-start | bytes 688136 | tf_op jit(solution)/shard_map/ppermute | solution.py:119
  213.9 12.5 %collective-permute-start.110 = (bf16[32,3584]{1,0:T(8,128)(2,1)S(1)}, bf16[32,3584]{1,0:T(8,128)(2,1)S(1)}, u32[]{:S(2)}, u32[]{:S(2)}) collective-permute-start(bf16[32,3584]{1,0:T(8,128)(2,1)S(1)} %add_convert_fusion.6), channel_id=1, source_target_pairs={{0,4},{1,5},{2,6},{3,7},{4,0},{5,1},{6,2},{7,3},{8,12},{9,13},{10,... | collective-permute-start | bytes 688136 | tf_op jit(solution)/shard_map/ppermute | solution.py:119
  215.1 11.3 %collective-permute-start.111 = (bf16[32,3584]{1,0:T(8,128)(2,1)S(1)}, bf16[32,3584]{1,0:T(8,128)(2,1)S(1)}, u32[]{:S(2)}, u32[]{:S(2)}) collective-permute-start(bf16[32,3584]{1,0:T(8,128)(2,1)S(1)} %add_convert_fusion.5), channel_id=1, source_target_pairs={{0,6},{1,7},{2,4},{3,5},{4,2},{5,3},{6,0},{7,1},{8,14},{9,15},{10,... | collective-permute-start | bytes 688136 | tf_op jit(solution)/shard_map/ppermute | solution.py:119
  228.8 9.6 %collective-permute-start.121 = (bf16[32,3584]{1,0:T(8,128)(2,1)}, bf16[32,3584]{1,0:T(8,128)(2,1)S(1)}, u32[]{:S(2)}, u32[]{:S(2)}) collective-permute-start(bf16[32,3584]{1,0:T(8,128)(2,1)} %add_convert_fusion.1), channel_id=1, source_target_pairs={{0,6},{1,7},{2,4},{3,5},{4,2},{5,3},{6,0},{7,1},{8,14},{9,15},{10,... | collective-permute-start | bytes 688136 | tf_op jit(solution)/shard_map/ppermute | solution.py:119
  231.0 11.5 %collective-permute-start.119 = (bf16[32,3584]{1,0:T(8,128)(2,1)}, bf16[32,3584]{1,0:T(8,128)(2,1)S(1)}, u32[]{:S(2)}, u32[]{:S(2)}) collective-permute-start(bf16[32,3584]{1,0:T(8,128)(2,1)} %add_convert_fusion.2), channel_id=1, source_target_pairs={{0,4},{1,5},{2,6},{3,7},{4,0},{5,1},{6,2},{7,3},{8,12},{9,13},{10,... | collective-permute-start | bytes 688136 | tf_op jit(solution)/shard_map/ppermute | solution.py:119
  233.3 9.2 %collective-permute-start.117 = (bf16[32,3584]{1,0:T(8,128)(2,1)}, bf16[32,3584]{1,0:T(8,128)(2,1)S(1)}, u32[]{:S(2)}, u32[]{:S(2)}) collective-permute-start(bf16[32,3584]{1,0:T(8,128)(2,1)} %add_convert_fusion.3), channel_id=1, source_target_pairs={{0,2},{1,3},{2,0},{3,1},{4,6},{5,7},{6,4},{7,5},{8,10},{9,11},{10,... | collective-permute-start | bytes 688136 | tf_op jit(solution)/shard_map/ppermute | solution.py:119
  (70 other events, 502.4 us)
